TPU v7x, 256 devices: a whole 4x4x8 slice. The times are simulated.
256 devices in a mesh: member: 4 (over z_lo, core), tile: 64 (over y, x, z_hi).
Axes of the slice: x: 4, y: 4, z: 8 (z_hi: 4, z_lo: 2; z = z_hi * 2 + z_lo), core: 2. Of those that a mesh axis runs over, the one named last changes fastest.
Arguments:
- member_predictions: bfloat16 [4, 80, 3072, 1536], P(None, 'member', 'tile'), may hold values from -5 to 13
- meridional_operator: float32 [384, 128], replicated, may hold values from -0.3125 to 0.3125
- zonal_operator: float32 [1024, 48], P('tile'), may hold values from -0.875 to 0.875
Outputs:
- coarse_anomalies: float32 [4, 80, 512, 1024], P(None, None, 'tile', 'member')
All inputs are finite; a program needn't handle non-finite values.
Results may differ from a plain program's by a relative error of at most 0.0003.
Values sent between devices are 32-bit elements; how exact they have to be, the bound alone decides.
No kernel may reach another device: no remote copies, remote signals or barrier semaphores. Data moves between devices by JAX's collectives and lax.ppermute only.
A program may use at most 128 MiB of HBM per device.

v0:
```python
import math

import jax
import jax.numpy as jnp
from jax import lax
from jax.sharding import PartitionSpec as P

M = 80


def coarsen_field(fields, meridional_operator, zonal_operator):
    levels = fields.shape[0]
    count = fields.shape[1]
    width = fields.shape[2]
    rows = fields.shape[3]
    block = meridional_operator.shape[0]
    flat_rows = fields.reshape(levels * count * width, rows)
    pieces = []
    for band in range(rows // block):
        section = flat_rows[:, band * block : (band + 1) * block]
        pieces.append(
            jnp.dot(
                section,
                meridional_operator,
                precision=lax.Precision.HIGHEST,
                preferred_element_type=jnp.float32,
            )
        )
    across = jnp.concatenate(pieces, axis=1).reshape(levels * count, width, rows // 3)
    result = jnp.einsum("cx,mxi->mic", zonal_operator, across, precision=lax.Precision.HIGHEST)
    return result.reshape(levels, count, rows // 3, zonal_operator.shape[0])


def body(member_predictions, meridional_operator, zonal_operator):
    scale = 1.0 / math.sqrt(M - 1)
    detailed_mesh = member_predictions.astype(jnp.float32)
    total = lax.psum(jnp.sum(detailed_mesh, axis=1, keepdims=True), "member")
    anomaly = (detailed_mesh - total / M) * scale
    reduced_mesh = coarsen_field(anomaly, meridional_operator, zonal_operator)
    reordered_rows = lax.all_to_all(
        lax.all_to_all(reduced_mesh, "tile", split_axis=2, concat_axis=3, tiled=True),
        "member",
        split_axis=3,
        concat_axis=1,
        tiled=True,
    )
    return reordered_rows


def solution(mesh):
    in_specs = (P(None, "member", "tile", None), P(), P("tile", None))
    out_specs = P(None, None, "tile", "member")
    return jax.shard_map(body, mesh=mesh, in_specs=in_specs, out_specs=out_specs, check_vma=False)
```

profile of v0, /device:TPU:32, one launch (start us, length us, event | category | flops | bytes accessed | tf_op | source)
XLA Modules:
  0.0 384.6 jit_solution(15289890878516518746)
XLA Ops:
  6.5 0.0 copy-start
  6.5 0.0 all-reduce.2.cloned.1.call-start
  6.5 7.6 %convert_reduce_fusion = f32[4,48,1536]{2,1,0:T(8,128)} fusion(bf16[4,20,48,1536]{3,2,1,0:T(8,128)(2,1)} %param.3), kind=kLoop, calls=%fused_computation.1 | loop fusion | flops 11501568 | bytes 12976128 | tf_op jit(solution)/shard_map/reduce_sum | solution.py:37
  14.1 0.0 all-reduce.2.cloned.1.call-update
  14.2 49.9 %all-reduce.2.cloned.1.call-done = f32[4,1,48,1536]{3,2,0,1:T(8,128)} async-done(((f32[4,1,48,1536]{3,2,0,1:T(8,128)}), f32[4,1,48,1536]{3,2,0,1:T(8,128)}) %all-reduce.2.cloned.1.call-update) | async-done | bytes 1179664 | tf_op jit(solution)/shard_map/psum | solution.py:37
  64.1 1.4 multiply_bitcast_fusion
  65.4 7.4 %fusion = f32[4,20,48,1536]{3,2,1,0:T(8,128)S(1)} fusion(bf16[4,20,48,1536]{3,2,1,0:T(8,128)(2,1)} %param.3, f32[4,48,1536]{2,1,0:T(8,128)S(1)} %multiply_bitcast_fusion), kind=kLoop, calls=%fused_computation.2 | loop fusion | flops 17694720 | bytes 36569088 | tf_op jit(solution)/shard_map/mul | solution.py:38
  72.8 0.0 copy-done
  72.8 5.4 %fusion.1 = f32[3840,128]{0,1:T(8,128)S(1)} fusion(f32[384,128]{1,0:T(8,128)S(1)} %copy-done, f32[3840,1536]{1,0:T(8,128)S(1)} %bitcast.30), kind=kOutput, calls=%fused_computation.4 | convolution fusion | flops 2264924160 | bytes 8060928 | tf_op jit(solution)/shard_map/dot_general | solution.py:22
  78.3 5.4 %fusion.3 = f32[3840,128]{0,1:T(8,128)S(1)} fusion(f32[384,128]{1,0:T(8,128)S(1)} %copy-done, f32[3840,1536]{1,0:T(8,128)S(1)} %bitcast.31), kind=kOutput, calls=%fused_computation.6 | convolution fusion | flops 2264924160 | bytes 8060928 | tf_op jit(solution)/shard_map/dot_general | solution.py:22
  83.7 5.8 %fusion.5 = f32[3840,128]{0,1:T(8,128)S(1)} fusion(f32[384,128]{1,0:T(8,128)S(1)} %copy-done, f32[3840,1536]{1,0:T(8,128)S(1)} %bitcast.32), kind=kOutput, calls=%fused_computation.8 | convolution fusion | flops 2264924160 | bytes 8060928 | tf_op jit(solution)/shard_map/dot_general | solution.py:22
  89.5 5.4 %fusion.7 = f32[3840,128]{0,1:T(8,128)S(1)} fusion(f32[384,128]{1,0:T(8,128)S(1)} %copy-done, f32[3840,1536]{1,0:T(8,128)S(1)} %bitcast.33), kind=kOutput, calls=%fused_computation.10 | convolution fusion | flops 2264924160 | bytes 8060928 | tf_op jit(solution)/shard_map/dot_general | solution.py:22
  94.9 3.4 pad_maximum_fusion
  98.3 0.0 copy-start.2
  98.3 9.1 %copy.19 = f32[3840,512]{1,0:T(8,128)} copy(f32[3840,512]{0,1:T(8,128)} %pad_maximum_fusion) | data formatting | bytes 15728640 | tf_op jit(solution)/shard_map/concatenate | solution.py:29
  107.4 0.0 copy-done.2
  107.4 6.5 %fusion.9 = f32[4,20,512,16]{2,3,1,0:T(8,128)S(1)} fusion(f32[4,20,512,48]{2,3,1,0:T(8,128)} %bitcast.38, f32[16,48]{1,0:T(8,128)S(1)} %copy-done.2), kind=kOutput, calls=%fused_computation.13 | convolution fusion | flops 377487360 | bytes 10488832 | tf_op jit(solution)/shard_map/cx,mxi->mic/dot_general | solution.py:30
  113.9 14.3 %copy.20 = f32[4,20,512,16]{1,3,0,2:T(8,128)} copy(f32[4,20,512,16]{2,3,1,0:T(8,128)S(1)} %fusion.9) | data formatting | bytes 5242880 | tf_op jit(solution)/shard_map/cx,mxi->mic/dot_general | solution.py:30
  128.2 19.0 %reshape.11 = f32[64,1,10240]{2,1,0:T(1,128)S(1)} reshape(f32[512,4,16,20]{3,2,1,0:T(8,128)} %bitcast.34) | data formatting | bytes 5242880
  147.2 78.5 %all_to_all.36 = f32[64,1,10240]{2,1,0:T(1,128)} all-to-all(f32[64,1,10240]{2,1,0:T(1,128)S(1)} %reshape.11), channel_id=1, replica_groups=mesh['member'=4,'tile'=64] {'tile'}, dimensions={0} | all-to-all | bytes 5242880 | tf_op jit(solution)/shard_map/all_to_all | solution.py:41
  225.7 0.5 broadcast.1
  226.2 8.6 %reduce = f32[64,10240]{1,0:T(8,128)S(1)} reduce(f32[64,1,10240]{2,1,0:T(1,128)} %all_to_all.36, f32[]{:T(128)} %broadcast.1), dimensions={1}, to_apply=%all_to_all.26.reduce_sub_computation | reduce | bytes 5242884 | tf_op jit(solution)/shard_map/all_to_all | solution.py:41
  234.8 20.9 %reshape.12 = f32[512,4,16,20]{3,2,1,0:T(8,128)} reshape(f32[64,10240]{1,0:T(8,128)S(1)} %reduce) | data formatting | bytes 5242880
  255.7 20.3 %copy.28 = f32[4,20,8,64,16]{1,2,0,4,3:T(8,128)} copy(f32[4,20,8,64,16]{1,4,0,2,3:T(8,128)} %bitcast.36) | data formatting | bytes 5242880 | tf_op jit(solution)/shard_map/all_to_all | solution.py:41
  276.1 21.1 %reshape.13 = f32[4,1,163840]{2,1,0:T(1,128)S(1)} reshape(f32[1024,4,8,20]{3,2,1,0:T(8,128)} %bitcast.37) | data formatting | bytes 5242880
  297.2 32.9 %all_to_all.37 = f32[4,1,163840]{2,1,0:T(1,128)} all-to-all(f32[4,1,163840]{2,1,0:T(1,128)S(1)} %reshape.13), channel_id=1, replica_groups=mesh['member'=4,'tile'=64] {'member'}, dimensions={0} | all-to-all | bytes 5242880 | tf_op jit(solution)/shard_map/all_to_all | solution.py:40
  330.0 9.2 %reduce.1 = f32[4,163840]{1,0:T(4,128)S(1)} reduce(f32[4,1,163840]{2,1,0:T(1,128)} %all_to_all.37, f32[]{:T(128)} %broadcast.1), dimensions={1}, to_apply=%all_to_all.30.reduce_sub_computation | reduce | bytes 5242884 | tf_op jit(solution)/shard_map/all_to_all | solution.py:40
  339.2 25.3 %reshape.14 = f32[1024,4,8,20]{3,2,1,0:T(8,128)} reshape(f32[4,163840]{1,0:T(4,128)S(1)} %reduce.1) | data formatting | bytes 5242880
  364.4 0.0 copy-start.1
  364.4 10.9 %copy.29 = f32[4,20,8,4,256]{4,3,2,1,0:T(4,128)S(1)} copy(f32[4,20,8,4,256]{1,2,0,4,3:T(8,128)} %bitcast.35) | data formatting | bytes 5242880 | tf_op jit(solution)/shard_map/all_to_all | solution.py:40
  375.3 2.0 copy.25
  377.3 0.0 copy-done.1
Async XLA Ops:
  6.5 66.3 %copy-start = (f32[384,128]{1,0:T(8,128)S(1)}, f32[384,128]{1,0:T(8,128)}, u32[]{:S(2)}) copy-start(f32[384,128]{1,0:T(8,128)} %param.4) | copy-start | bytes 589828
  6.5 57.5 %all-reduce.2.cloned.1.call-start = ((), (), s32[]{:S(2)}) async-start(), calls=%async_computation.2 | async-start | bytes 2359296 | tf_op jit(solution)/shard_map/psum | solution.py:37
  98.3 9.1 %copy-start.2 = (f32[16,48]{1,0:T(8,128)S(1)}, f32[16,48]{1,0:T(8,128)}, u32[]{:S(2)}) copy-start(f32[16,48]{1,0:T(8,128)} %param.5) | copy-start | bytes 9220
  364.4 12.8 %copy-start.1 = (f32[384,128]{1,0:T(8,128)S(1)}, f32[384,128]{1,0:T(8,128)}, u32[]{:S(2)}) copy-start(f32[384,128]{1,0:T(8,128)} %param.4) | copy-start | bytes 589828
Sparse Core Ops, SparseCore 0:
  14.3 49.7 all-reduce.1
where the time goes:
time: 390 us; the launch traced here: 385 us
  local copies, waits for them, and re-layouts  143 us (37%)
  blocking collectives  111 us (28%)
  waiting for transfers between devices  49.9 us (13%)
  other arithmetic  37.5 us (10%)
  matrix products  28.5 us (7%)
  between operations  13.9 us (4%)
    unnamed x10, local copies, waits for them, and re-layouts  86.3 us
    all_to_all x1, blocking collectives, body(): lax.all_to_all(reduced_mesh, 'tile', split_axis=2, concat_axis=3, tiled=T...  78.5 us
    psum x1, waiting for transfers between devices, body(): total = lax.psum(jnp.sum(detailed_mesh, axis=1, keepdims=True), 'member')  49.9 us
    all_to_all x1, blocking collectives, body(): lax.all_to_all(lax.all_to_all(reduced_mesh, 'tile', split_axis=2, concat_...  32.9 us
    dot_general x4, matrix products, coarsen_field(): jnp.dot(section, meridional_operator, precision=lax.Precision.HIGHEST, pr...  22.1 us
    all_to_all x2, local copies, waits for them, and re-layouts, body(): lax.all_to_all(reduced_mesh, 'tile', split_axis=2, concat_axis=3, tiled=T...  20.8 us
    dot_general x1, local copies, waits for them, and re-layouts, coarsen_field(): jnp.einsum('cx,mxi->mic', zonal_operator, across, precision=lax.Precision...  14.3 us
    all_to_all x2, local copies, waits for them, and re-layouts, body(): lax.all_to_all(lax.all_to_all(reduced_mesh, 'tile', split_axis=2, concat_...  12.8 us
  transfers between devices with their start and end apart: 1, of which 1 were waited for; matrix products, arithmetic and copies ran while one was open for 0% of the time, Pallas kernels for 0%

commit v1 on v0

v1 whole, which is shorter than its diff:
```python
import functools
import math

import jax
import jax.numpy as jnp
from jax import lax
from jax.experimental import pallas as pl
from jax.experimental.pallas import tpu as pltpu
from jax.sharding import Mesh
from jax.sharding import PartitionSpec as P

M = 80
AX = ("zlo", "core", "y", "x", "zhi")
PAIRS = 8
ROWS = 384
CUT, GROUPS = 4, 10
ANY = pl.BlockSpec(memory_space=pl.ANY)


def split2(v):
    hi = v.astype(jnp.bfloat16)
    return hi, (v - hi.astype(jnp.float32)).astype(jnp.bfloat16)


def restrict_kernel(first, count, x_ref, mer_ref, zon_ref, *rest):
    outs, (buf, mer_buf, zon_buf, stage, in_sems, op_sems, out_sems) = rest[:4], rest[4:]
    base = lax.axis_index("y")

    def load(g, j):
        rows = pl.ds((first + g) * ROWS, ROWS)
        lane = pl.multiple_of((base ^ j) * ROWS, 128)
        to = buf.at[g, :, pl.ds(j * ROWS, ROWS)]
        return pltpu.make_async_copy(x_ref.at[rows, pl.ds(lane, ROWS)], to, in_sems.at[g, j])

    def store(g, j):
        lanes = pl.ds(128 * g, 128)
        return pltpu.make_async_copy(stage.at[j, :, :, lanes], outs[j].at[:, :, lanes], out_sems.at[g, j])

    get_mer = pltpu.make_async_copy(mer_ref, mer_buf, op_sems.at[0])
    get_zon = pltpu.make_async_copy(zon_ref, zon_buf, op_sems.at[1])
    get_zon.start()
    get_mer.start()
    for g in range(count):
        for j in range(4):
            load(g, j).start()
    k = lax.broadcasted_iota(jnp.int32, (48, 192), 0)
    n = lax.broadcasted_iota(jnp.int32, (48, 192), 1)
    spread = jnp.where(lax.rem(n, 48) == k, 1.0, 0.0).astype(jnp.bfloat16)
    row = lax.broadcasted_iota(jnp.int32, (64, 192), 0)
    col = lax.broadcasted_iota(jnp.int32, (64, 192), 1) - 48 * lax.shift_right_logical(row, 4)
    keep = (col >= 0) & (col < 48)
    get_zon.wait()
    tiles = []
    for part in split2(zon_buf[...]):
        wide = jnp.dot(part, spread, preferred_element_type=jnp.float32)
        wide = jnp.concatenate([wide] * 4, axis=0)
        tiles.append(jnp.where(keep, wide, 0.0).astype(jnp.bfloat16))
    zon = jnp.concatenate(tiles, axis=0)
    get_mer.wait()
    mer = jnp.concatenate(split2(mer_buf[...]), axis=1)

    for g in range(count):
        for j in range(4):
            load(g, j).wait()
        w = []
        for q in range(2):
            t = jnp.dot(zon, buf[g, 192 * q : 192 * q + 192], preferred_element_type=jnp.float32)
            w.append(t[:64] + t[64:])
        w = jnp.concatenate(split2(jnp.concatenate(w, axis=0)), axis=0)
        for j in range(4):
            v = jnp.dot(w[:, j * ROWS : (j + 1) * ROWS], mer, preferred_element_type=jnp.float32)
            v = (v[128:, 128:] + v[128:, :128]) + v[:128, 128:] + v[:128, :128]
            stage[j, :, :, 128 * g : 128 * g + 128] = v.T.reshape(16, 8, 128)
            store(g, j).start()
    for g in range(count):
        for j in range(4):
            store(g, j).wait()


def restrict(x, mer, zon, first, count):
    lanes = count * 128
    return pl.pallas_call(
        functools.partial(restrict_kernel, first, count),
        out_shape=[jax.ShapeDtypeStruct((16, 8, lanes), jnp.float32)] * 4,
        in_specs=[ANY] * 3,
        out_specs=[ANY] * 4,
        scratch_shapes=[
            pltpu.VMEM((count, ROWS, 4 * ROWS), jnp.bfloat16),
            pltpu.VMEM(mer.shape, jnp.float32),
            pltpu.VMEM(zon.shape, jnp.float32),
            pltpu.VMEM((4, 16, 8, lanes), jnp.float32),
            pltpu.SemaphoreType.DMA((count, 4)),
            pltpu.SemaphoreType.DMA((2,)),
            pltpu.SemaphoreType.DMA((count, 4)),
        ],
        compiler_params=pltpu.CompilerParams(vmem_limit_bytes=56 * 2**20),
        cost_estimate=pl.CostEstimate(
            flops=count * 800_000_000, bytes_accessed=count * ROWS * ROWS * 16, transcendentals=0
        ),
        name=f"restrict_{first}",
    )(x, mer, zon)


def swap_groups(v):
    group = lax.shift_right_logical(lax.broadcasted_iota(jnp.int32, (8, 128), 1), 4)
    for d in (4, 2, 1):
        low = (group & d) == 0
        new = list(v)
        for i in range(8):
            if i & d:
                continue
            a, b = v[i], v[i + d]
            if d == 4:
                c = pltpu.roll(jnp.where(low, b, a), 64, 1)
                new[i], new[i + d] = jnp.where(low, a, c), jnp.where(low, c, b)
            else:
                new[i] = jnp.where(low, a, pltpu.roll(b, 16 * d, 1))
                new[i + d] = jnp.where(low, pltpu.roll(a, 128 - 16 * d, 1), b)
        v = new
    return v


def finish_kernel(levels, tiles1, tiles2, *refs):
    refs = list(refs)
    r1 = refs.pop(0)
    r2 = refs.pop(0) if tiles2 else None
    if tiles2:
        refs.pop(0)
    out, b1, b2, stage, in_sems, out_sems = refs
    y = lax.axis_index("y")
    wide1 = pl.ds(128 * tiles1[0], 128 * len(tiles1))

    def loads(h):
        rows = pl.ds(8 * h, 8)
        found = [pltpu.make_async_copy(r1.at[:, rows, :, wide1], b1.at[:, rows], in_sems.at[h, 0])]
        if tiles2:
            found.append(pltpu.make_async_copy(r2.at[:, rows], b2.at[:, rows], in_sems.at[h, 1]))
        return found

    def store(h, n):
        lanes = pl.ds(128 * h, 128)
        return pltpu.make_async_copy(stage.at[n, :, :, lanes], out.at[levels[n], :, :, lanes], out_sems.at[h, n])

    for h in range(2):
        for c in loads(h):
            c.start()
    scale = 1.0 / math.sqrt(M - 1)
    for h in range(2):
        for c in loads(h):
            c.wait()
        lanes = slice(128 * h, 128 * h + 128)

        def shuffle(k, sums):
            sums = list(sums)
            p = y ^ k
            for tile in (*tiles1, *tiles2):
                if tile < CUT:
                    at = 128 * (tile - tiles1[0])
                    v = [b1[k, 8 * h + i, :, at : at + 128] for i in range(8)]
                else:
                    at = 128 * (tile - CUT)
                    v = [b2[k, 8 * h + i, :, at : at + 128] for i in range(8)]
                v = swap_groups(v)
                for i in range(8):
                    level, m = divmod(8 * tile + i, 20)
                    if level in levels:
                        n = level - levels[0]
                        stage[n, p * 20 + m, :, lanes] = v[i]
                        sums[n] = sums[n] + v[i]
            return tuple(sums)

        zero = jnp.zeros((8, 128), jnp.float32)
        sums = lax.fori_loop(0, 4, shuffle, (zero,) * len(levels))
        for n in range(len(levels)):
            mean = sums[n] / M

            def centre(q, _):
                for m in range(20):
                    stage[n, q * 20 + m, :, lanes] = (stage[n, q * 20 + m, :, lanes] - mean) * scale
                return 0

            lax.fori_loop(0, 4, centre, 0)
            store(h, n).start()
    for h in range(2):
        for n in range(len(levels)):
            store(h, n).wait()


def finish(levels, r1, r2, earlier):
    first, last = 20 * levels[0] // PAIRS, (20 * levels[-1] + 19) // PAIRS
    tiles1 = tuple(range(first, min(last + 1, CUT)))
    tiles2 = tuple(range(CUT, last + 1))
    operands, aliases = [r1], {}
    if tiles2:
        operands, aliases = [r1, r2, earlier], {2: 0}
    return pl.pallas_call(
        functools.partial(finish_kernel, levels, tiles1, tiles2),
        out_shape=jax.ShapeDtypeStruct((4, M, 8, 256), jnp.float32),
        in_specs=[ANY] * len(operands),
        out_specs=ANY,
        input_output_aliases=aliases,
        scratch_shapes=[
            pltpu.VMEM((4, 16, 8, 128 * len(tiles1)), jnp.float32),
            pltpu.VMEM((4, 16, 8, 128 * max(1, len(tiles2))), jnp.float32),
            pltpu.VMEM((len(levels), M, 8, 256), jnp.float32),
            pltpu.SemaphoreType.DMA((2, 2)),
            pltpu.SemaphoreType.DMA((2, len(levels))),
        ],
        compiler_params=pltpu.CompilerParams(vmem_limit_bytes=16 * 2**20),
        cost_estimate=pl.CostEstimate(
            flops=len(levels) * 2_000_000, bytes_accessed=len(levels) * 1_300_000, transcendentals=0
        ),
        name=f"finish_{levels[0]}",
    )(*operands)


def swap_y(k):
    return [(a * 64 + y * 16 + b, a * 64 + (y ^ k) * 16 + b) for a in range(4) for y in range(4) for b in range(16)]


def planes():
    return [[(y ^ j) * 64 + y * 16 + b for j in range(4) for b in range(16)] for y in range(4)]


def along_y(parts):
    return jnp.concatenate([parts[0]] + [lax.ppermute(parts[k], AX, swap_y(k)) for k in (1, 2, 3)], axis=0)


def across_plane(v):
    return lax.all_to_all(v, AX, 0, 0, axis_index_groups=planes(), tiled=True).reshape(4, 16, 8, -1)


def body(member_predictions, meridional_operator, zonal_operator):
    x = member_predictions.reshape(-1, member_predictions.shape[-1])
    ops = (meridional_operator, zonal_operator)
    one = along_y(restrict(x, *ops, 0, CUT))
    two = restrict(x, *ops, CUT, GROUPS - CUT)
    one, *two = lax.optimization_barrier((one, *two))
    one, two = across_plane(one), across_plane(along_y(two))
    return finish((1, 2, 3), one, two, finish((0,), one, None, None))


def solution(mesh):
    fine = Mesh(mesh.devices.reshape(2, 2, 4, 4, 4), AX)
    member, tile = ("zlo", "core"), ("y", "x", "zhi")
    in_specs = (P(None, member, tile, None), P(), P(tile, None))
    out_specs = P(None, None, tile, member)
    return jax.shard_map(body, mesh=fine, in_specs=in_specs, out_specs=out_specs, check_vma=False)
```

time: 390 us -> 117 us (0.30); the launches traced: 385 us -> 116 us
  local copies, waits for them, and re-layouts: 143 us -> 0.02 us
  blocking collectives: 111 us -> 0 us
  other arithmetic: 37.5 us -> 2.32 us
  matrix products: 28.5 us -> 0 us
  starting transfers between devices: 0.01 us -> 26.8 us
  Pallas kernels: 0 us -> 21.6 us
  waiting for transfers between devices: 49.9 us -> 65.6 us
  between operations: 13.9 us -> 0.09 us
    all_to_all x2 -> x0, blocking collectives: 111 us -> none  [the longest x1 78.5 us: body(): lax.all_to_all(reduced_mesh, 'tile', split_axis=2, concat_axis=3, tiled=T...]
    unnamed x10, local copies, waits for them, and re-layouts: 86.3 us -> 0.02 us
    psum x1 -> x0, waiting for transfers between devices: 49.9 us -> none  [body(): total = lax.psum(jnp.sum(detailed_mesh, axis=1, keepdims=True), 'member')]
    all_to_all x0 -> x2, waiting for transfers between devices: none -> 42.7 us  [across_plane(): lax.all_to_all(v, AX, 0, 0, axis_index_groups=planes(), tiled=True)]
    all_to_all x4 -> x0, local copies, waits for them, and re-layouts: 33.6 us -> none  [the longest x2 20.8 us: body(): lax.all_to_all(reduced_mesh, 'tile', split_axis=2, concat_axis=3, tiled=T...]
    dot_general x5 -> x0, matrix products: 28.5 us -> none  [the longest x4 22.1 us: coarsen_field(): jnp.dot(section, meridional_operator, precision=lax.Precision.HIGHEST, pr...]
    ppermute x0 -> x6, waiting for transfers between devices: none -> 22.9 us  [along_y(): lax.ppermute(parts[k], AX, swap_y(k))]
    pallas_call x0 -> x4, Pallas kernels: none -> 21.6 us  [the longest x2 15.1 us: restrict(): pl.pallas_call(functools.partial(restrict_kernel, first, count), out_shap...]
  transfers between devices with their start and end apart: 1 -> 8, of which waited for: 1 -> 7; matrix products, arithmetic and copies ran while one was open for 0% -> 1% of each run, Pallas kernels for 0% -> 10%
where the time goes in v1:
time: 117 us; the launch traced here: 116 us
  waiting for transfers between devices  65.6 us (56%)
  starting transfers between devices  26.8 us (23%)
  Pallas kernels  21.6 us (18%)
  other arithmetic  2.32 us (2%)
    all_to_all x2, waiting for transfers between devices, across_plane(): lax.all_to_all(v, AX, 0, 0, axis_index_groups=planes(), tiled=True)  42.7 us
    ppermute x6, waiting for transfers between devices, along_y(): lax.ppermute(parts[k], AX, swap_y(k))  22.9 us
    all_to_all x2, starting transfers between devices, across_plane(): lax.all_to_all(v, AX, 0, 0, axis_index_groups=planes(), tiled=True)  17.2 us
    pallas_call x2, Pallas kernels, restrict(): pl.pallas_call(functools.partial(restrict_kernel, first, count), out_shap...  15.1 us
    ppermute x6, starting transfers between devices, along_y(): lax.ppermute(parts[k], AX, swap_y(k))  9.56 us
    pallas_call x2, Pallas kernels, finish(): pl.pallas_call(functools.partial(finish_kernel, levels, tiles1, tiles2),...  6.5 us
  transfers between devices with their start and end apart: 8, of which 7 were waited for; matrix products, arithmetic and copies ran while one was open for 1% of the time, Pallas kernels for 10%

profile of v1, /device:TPU:32, one launch (start us, length us, event | category | flops | bytes accessed | tf_op | source)
XLA Modules:
  0.0 116.3 jit_solution(12781107930245098171)
XLA Ops:
  0.0 6.3 %restrict_0.1 = (f32[16,8,512]{2,1,0:T(8,128)}, f32[16,8,512]{2,1,0:T(8,128)}, f32[16,8,512]{2,1,0:T(8,128)}, f32[16,8,512]{2,1,0:T(8,128)}) custom-call(bf16[3840,1536]{1,0:T(8,128)(2,1)} %bitcast.6, f32[384,128]{1,0:T(8,128)} %mer_ref.3, f32[16,48]{1,0:T(8,128)} %zon_ref.3), custom_call_target="tpu_custom_call" | custom-call | flops 3200000000 | bytes 9437184 | tf_op jit(solution)/shard_map/restrict_0/pallas_call | solution.py:82
  6.3 1.7 %collective-permute-start = (f32[16,8,512]{2,1,0:T(8,128)}, f32[16,8,512]{2,1,0:T(8,128)S(1)}, u32[]{:S(2)}, u32[]{:S(2)}) collective-permute-start(f32[16,8,512]{2,1,0:T(8,128)} %get-tuple-element.19), channel_id=1, source_target_pairs={{0,16},{1,17},{2,18},{3,19},{4,20},{5,21},{6,22},{7,23},{8,24},{9,... | collective-permute-start | bytes 786440 | tf_op jit(solution)/shard_map/ppermute | solution.py:226
  8.0 2.9 %collective-permute-start.1 = (f32[16,8,512]{2,1,0:T(8,128)}, f32[16,8,512]{2,1,0:T(8,128)S(1)}, u32[]{:S(2)}, u32[]{:S(2)}) collective-permute-start(f32[16,8,512]{2,1,0:T(8,128)} %get-tuple-element.20), channel_id=1, source_target_pairs={{0,32},{1,33},{2,34},{3,35},{4,36},{5,37},{6,38},{7,39},{8,40},{9,... | collective-permute-start | bytes 786440 | tf_op jit(solution)/shard_map/ppermute | solution.py:226
  10.9 0.0 copy-start.1
  10.9 0.2 collective-permute-start.2
  11.1 8.7 %restrict_4.1 = (f32[16,8,768]{2,1,0:T(8,128)}, f32[16,8,768]{2,1,0:T(8,128)}, f32[16,8,768]{2,1,0:T(8,128)}, f32[16,8,768]{2,1,0:T(8,128)}) custom-call(bf16[3840,1536]{1,0:T(8,128)(2,1)} %bitcast.7, f32[384,128]{1,0:T(8,128)} %mer_ref.3, f32[16,48]{1,0:T(8,128)} %zon_ref.3), custom_call_target="tpu_custom_call" | custom-call | flops 4800000000 | bytes 14155776 | tf_op jit(solution)/shard_map/restrict_4/pallas_call | solution.py:82
  19.9 0.0 collective-permute-done
  19.9 3.0 %collective-permute-done.1 = f32[16,8,512]{2,1,0:T(8,128)S(1)} collective-permute-done((f32[16,8,512]{2,1,0:T(8,128)}, f32[16,8,512]{2,1,0:T(8,128)S(1)}, u32[]{:S(2)}, u32[]{:S(2)}) %collective-permute-start.1) | collective-permute-done | bytes 262176 | tf_op jit(solution)/shard_map/ppermute | solution.py:226
  22.8 2.6 %collective-permute-done.2 = f32[16,8,512]{2,1,0:T(8,128)S(1)} collective-permute-done((f32[16,8,512]{2,1,0:T(8,128)}, f32[16,8,512]{2,1,0:T(8,128)S(1)}, u32[]{:S(2)}, u32[]{:S(2)}) %collective-permute-start.2) | collective-permute-done | bytes 262176 | tf_op jit(solution)/shard_map/ppermute | solution.py:226
  25.4 0.0 copy-done.1
  25.4 1.0 pad_maximum_fusion.1
  26.5 0.0 copy-start.4
  26.5 0.0 copy-start.3
  26.5 0.0 copy-start.2
  26.5 0.0 copy-start
  26.5 11.9 %all-to-all-start = ((f32[64,8,512]{2,1,0:T(8,128)}), f32[64,8,512]{2,1,0:T(8,128)S(1)}, u32[]{:S(2)}, u32[]{:S(2)}) async-start(f32[64,8,512]{2,1,0:T(8,128)} %pad_maximum_fusion.1), calls=%async_computation | async-start | bytes 2097152 | tf_op jit(solution)/shard_map/all_to_all | solution.py:230
  38.4 0.0 copy-done.4
  38.4 0.1 collective-permute-start.3
  38.5 0.0 copy-done.3
  38.5 0.7 collective-permute-start.4
  39.2 0.0 copy-done.2
  39.2 4.0 %collective-permute-start.5 = (f32[16,8,768]{2,1,0:T(8,128)S(1)}, f32[16,8,768]{2,1,0:T(8,128)S(1)}, u32[]{:S(2)}, u32[]{:S(2)}) collective-permute-start(f32[16,8,768]{2,1,0:T(8,128)S(1)} %copy-done.2), channel_id=1, source_target_pairs={{0,48},{1,49},{2,50},{3,51},{4,52},{5,53},{6,54},{7,55},{8,56},{9,... | collective-permute-start | bytes 1179656 | tf_op jit(solution)/shard_map/ppermute | solution.py:226
  43.2 7.2 %collective-permute-done.3 = f32[16,8,768]{2,1,0:T(8,128)S(1)} collective-permute-done((f32[16,8,768]{2,1,0:T(8,128)S(1)}, f32[16,8,768]{2,1,0:T(8,128)S(1)}, u32[]{:S(2)}, u32[]{:S(2)}) %collective-permute-start.3) | collective-permute-done | bytes 393248 | tf_op jit(solution)/shard_map/ppermute | solution.py:226
  50.4 6.7 %collective-permute-done.4 = f32[16,8,768]{2,1,0:T(8,128)S(1)} collective-permute-done((f32[16,8,768]{2,1,0:T(8,128)S(1)}, f32[16,8,768]{2,1,0:T(8,128)S(1)}, u32[]{:S(2)}, u32[]{:S(2)}) %collective-permute-start.4) | collective-permute-done | bytes 393248 | tf_op jit(solution)/shard_map/ppermute | solution.py:226
  57.1 3.4 %collective-permute-done.5 = f32[16,8,768]{2,1,0:T(8,128)S(1)} collective-permute-done((f32[16,8,768]{2,1,0:T(8,128)S(1)}, f32[16,8,768]{2,1,0:T(8,128)S(1)}, u32[]{:S(2)}, u32[]{:S(2)}) %collective-permute-start.5) | collective-permute-done | bytes 393248 | tf_op jit(solution)/shard_map/ppermute | solution.py:226
  60.5 0.0 copy-done
  60.5 1.3 %pad_maximum_fusion = f32[64,8,768]{2,1,0:T(8,128)} fusion(f32[16,8,768]{2,1,0:T(8,128)S(1)} %collective-permute-done.5, f32[16,8,768]{2,1,0:T(8,128)S(1)} %collective-permute-done.4, f32[16,8,768]{2,1,0:T(8,128)S(1)} %collective-permute-done.3, f32[16,8,768]{2,1,0:T(8,128)S(1)} %copy-done), kind=kLoop, calls=%fused_computation | loop fusion | flops 1179648 | bytes 3145728 | tf_op jit(solution)/shard_map/concatenate | solution.py:226
  61.8 5.6 %all-to-all-done = f32[64,8,512]{2,1,0:T(8,128)S(1)} async-done(((f32[64,8,512]{2,1,0:T(8,128)}), f32[64,8,512]{2,1,0:T(8,128)S(1)}, u32[]{:S(2)}, u32[]{:S(2)}) %all-to-all-start) | async-done | bytes 1048608 | tf_op jit(solution)/shard_map/all_to_all | solution.py:230
  67.5 5.3 %all-to-all-start.1 = ((f32[64,8,768]{2,1,0:T(8,128)}), f32[64,8,768]{2,1,0:T(8,128)S(1)}, u32[]{:S(2)}, u32[]{:S(2)}) async-start(f32[64,8,768]{2,1,0:T(8,128)} %pad_maximum_fusion), calls=%async_computation.1 | async-start | bytes 3145728 | tf_op jit(solution)/shard_map/all_to_all | solution.py:230
  72.8 2.8 %finish_0.1.refs_2_ = f32[4,80,8,256]{3,2,1,0:T(8,128)} custom-call(f32[4,16,8,512]{3,2,1,0:T(8,128)S(1)} %bitcast.3), custom_call_target="tpu_custom_call" | custom-call | flops 2000000 | bytes 1300000 | tf_op jit(solution)/shard_map/finish_0/pallas_call | solution.py:196
  75.6 37.0 %all-to-all-done.1 = f32[64,8,768]{2,1,0:T(8,128)S(1)} async-done(((f32[64,8,768]{2,1,0:T(8,128)}), f32[64,8,768]{2,1,0:T(8,128)S(1)}, u32[]{:S(2)}, u32[]{:S(2)}) %all-to-all-start.1) | async-done | bytes 1572896 | tf_op jit(solution)/shard_map/all_to_all | solution.py:230
  112.6 3.7 %finish_1.1 = f32[4,80,8,256]{3,2,1,0:T(8,128)} custom-call(f32[4,16,8,512]{3,2,1,0:T(8,128)S(1)} %bitcast.4, f32[4,16,8,768]{3,2,1,0:T(8,128)S(1)} %bitcast.5, f32[4,80,8,256]{3,2,1,0:T(8,128)} %finish_0.1.refs_2_), custom_call_target="tpu_custom_call", output_to_operand_aliasing={{}: (2, {})} | custom-call | flops 6000000 | bytes 3900000 | tf_op jit(solution)/shard_map/finish_1/pallas_call | solution.py:196
Async XLA Ops:
  6.3 13.5 %collective-permute-start = (f32[16,8,512]{2,1,0:T(8,128)}, f32[16,8,512]{2,1,0:T(8,128)S(1)}, u32[]{:S(2)}, u32[]{:S(2)}) collective-permute-start(f32[16,8,512]{2,1,0:T(8,128)} %get-tuple-element.19), channel_id=1, source_target_pairs={{0,16},{1,17},{2,18},{3,19},{4,20},{5,21},{6,22},{7,23},{8,24},{9,... | collective-permute-start | bytes 786440 | tf_op jit(solution)/shard_map/ppermute | solution.py:226
  8.0 14.8 %collective-permute-start.1 = (f32[16,8,512]{2,1,0:T(8,128)}, f32[16,8,512]{2,1,0:T(8,128)S(1)}, u32[]{:S(2)}, u32[]{:S(2)}) collective-permute-start(f32[16,8,512]{2,1,0:T(8,128)} %get-tuple-element.20), channel_id=1, source_target_pairs={{0,32},{1,33},{2,34},{3,35},{4,36},{5,37},{6,38},{7,39},{8,40},{9,... | collective-permute-start | bytes 786440 | tf_op jit(solution)/shard_map/ppermute | solution.py:226
  10.9 14.5 %copy-start.1 = (f32[16,8,512]{2,1,0:T(8,128)S(1)}, f32[16,8,512]{2,1,0:T(8,128)}, u32[]{:S(2)}) copy-start(f32[16,8,512]{2,1,0:T(8,128)} %get-tuple-element.18) | copy-start | bytes 786436
  10.9 14.5 %collective-permute-start.2 = (f32[16,8,512]{2,1,0:T(8,128)}, f32[16,8,512]{2,1,0:T(8,128)S(1)}, u32[]{:S(2)}, u32[]{:S(2)}) collective-permute-start(f32[16,8,512]{2,1,0:T(8,128)} %get-tuple-element.21), channel_id=1, source_target_pairs={{0,48},{1,49},{2,50},{3,51},{4,52},{5,53},{6,54},{7,55},{8,56},{9,... | collective-permute-start | bytes 786440 | tf_op jit(solution)/shard_map/ppermute | solution.py:226
  26.5 11.9 %copy-start.4 = (f32[16,8,768]{2,1,0:T(8,128)S(1)}, f32[16,8,768]{2,1,0:T(8,128)}, u32[]{:S(2)}) copy-start(f32[16,8,768]{2,1,0:T(8,128)} %get-tuple-element.28) | copy-start | bytes 1179652
  26.5 12.0 %copy-start.3 = (f32[16,8,768]{2,1,0:T(8,128)S(1)}, f32[16,8,768]{2,1,0:T(8,128)}, u32[]{:S(2)}) copy-start(f32[16,8,768]{2,1,0:T(8,128)} %get-tuple-element.29) | copy-start | bytes 1179652
  26.5 12.7 %copy-start.2 = (f32[16,8,768]{2,1,0:T(8,128)S(1)}, f32[16,8,768]{2,1,0:T(8,128)}, u32[]{:S(2)}) copy-start(f32[16,8,768]{2,1,0:T(8,128)} %get-tuple-element.30) | copy-start | bytes 1179652
  26.5 34.1 %copy-start = (f32[16,8,768]{2,1,0:T(8,128)S(1)}, f32[16,8,768]{2,1,0:T(8,128)}, u32[]{:S(2)}) copy-start(f32[16,8,768]{2,1,0:T(8,128)} %get-tuple-element.27) | copy-start | bytes 1179652
  26.5 41.0 %all-to-all-start = ((f32[64,8,512]{2,1,0:T(8,128)}), f32[64,8,512]{2,1,0:T(8,128)S(1)}, u32[]{:S(2)}, u32[]{:S(2)}) async-start(f32[64,8,512]{2,1,0:T(8,128)} %pad_maximum_fusion.1), calls=%async_computation | async-start | bytes 2097152 | tf_op jit(solution)/shard_map/all_to_all | solution.py:230
  38.4 12.0 %collective-permute-start.3 = (f32[16,8,768]{2,1,0:T(8,128)S(1)}, f32[16,8,768]{2,1,0:T(8,128)S(1)}, u32[]{:S(2)}, u32[]{:S(2)}) collective-permute-start(f32[16,8,768]{2,1,0:T(8,128)S(1)} %copy-done.4), channel_id=1, source_target_pairs={{0,16},{1,17},{2,18},{3,19},{4,20},{5,21},{6,22},{7,23},{8,24},{9,... | collective-permute-start | bytes 1179656 | tf_op jit(solution)/shard_map/ppermute | solution.py:226
  38.5 18.6 %collective-permute-start.4 = (f32[16,8,768]{2,1,0:T(8,128)S(1)}, f32[16,8,768]{2,1,0:T(8,128)S(1)}, u32[]{:S(2)}, u32[]{:S(2)}) collective-permute-start(f32[16,8,768]{2,1,0:T(8,128)S(1)} %copy-done.3), channel_id=1, source_target_pairs={{0,32},{1,33},{2,34},{3,35},{4,36},{5,37},{6,38},{7,39},{8,40},{9,... | collective-permute-start | bytes 1179656 | tf_op jit(solution)/shard_map/ppermute | solution.py:226
  39.2 21.4 %collective-permute-start.5 = (f32[16,8,768]{2,1,0:T(8,128)S(1)}, f32[16,8,768]{2,1,0:T(8,128)S(1)}, u32[]{:S(2)}, u32[]{:S(2)}) collective-permute-start(f32[16,8,768]{2,1,0:T(8,128)S(1)} %copy-done.2), channel_id=1, source_target_pairs={{0,48},{1,49},{2,50},{3,51},{4,52},{5,53},{6,54},{7,55},{8,56},{9,... | collective-permute-start | bytes 1179656 | tf_op jit(solution)/shard_map/ppermute | solution.py:226
  67.5 45.2 %all-to-all-start.1 = ((f32[64,8,768]{2,1,0:T(8,128)}), f32[64,8,768]{2,1,0:T(8,128)S(1)}, u32[]{:S(2)}, u32[]{:S(2)}) async-start(f32[64,8,768]{2,1,0:T(8,128)} %pad_maximum_fusion), calls=%async_computation.1 | async-start | bytes 3145728 | tf_op jit(solution)/shard_map/all_to_all | solution.py:230

commit v2 on v1

v2 whole, which is shorter than its diff:
```python
import functools
import math

import jax
import jax.numpy as jnp
from jax import lax
from jax.experimental import pallas as pl
from jax.experimental.pallas import tpu as pltpu
from jax.sharding import Mesh
from jax.sharding import PartitionSpec as P

M = 80
AX = ("zlo", "core", "y", "x", "zhi")
PAIRS = 8
ROWS = 384
CUT, GROUPS = 4, 10
ANY = pl.BlockSpec(memory_space=pl.ANY)


def split2(v):
    hi = v.astype(jnp.bfloat16)
    return hi, (v - hi.astype(jnp.float32)).astype(jnp.bfloat16)


def own_member():
    return 2 * lax.axis_index("zlo") + lax.axis_index("core")


def restrict_kernel(first, count, along_y, x_ref, mer_ref, zon_ref, *rest):
    outs, (buf, mid, mer_buf, zon_buf, stage, in_sems, op_sems, out_sems) = rest[:4], rest[4:]
    base = lax.axis_index("y")
    at_x, at_z = lax.axis_index("x"), lax.axis_index("zhi")

    def load(g, j):
        rows = pl.ds((first + g) * ROWS, ROWS)
        lane = pl.multiple_of((base ^ j) * ROWS, 128)
        to = buf.at[g, :, pl.ds(j * ROWS, ROWS)]
        return pltpu.make_async_copy(x_ref.at[rows, pl.ds(lane, ROWS)], to, in_sems.at[g, j])

    def store(j):
        return pltpu.make_async_copy(stage.at[j], outs[j], out_sems.at[j])

    get_mer = pltpu.make_async_copy(mer_ref, mer_buf, op_sems.at[0])
    get_zon = pltpu.make_async_copy(zon_ref, zon_buf, op_sems.at[1])
    get_zon.start()
    get_mer.start()
    for g in range(count):
        for j in range(4):
            load(g, j).start()
    k = lax.broadcasted_iota(jnp.int32, (48, 192), 0)
    n = lax.broadcasted_iota(jnp.int32, (48, 192), 1)
    spread = jnp.where(lax.rem(n, 48) == k, 1.0, 0.0).astype(jnp.bfloat16)
    row = lax.broadcasted_iota(jnp.int32, (64, 192), 0)
    col = lax.broadcasted_iota(jnp.int32, (64, 192), 1) - 48 * lax.shift_right_logical(row, 4)
    keep = (col >= 0) & (col < 48)
    get_zon.wait()
    tiles = []
    for part in split2(zon_buf[...]):
        wide = jnp.dot(part, spread, preferred_element_type=jnp.float32)
        wide = jnp.concatenate([wide] * 4, axis=0)
        tiles.append(jnp.where(keep, wide, 0.0).astype(jnp.bfloat16))
    zon = jnp.concatenate(tiles, axis=0)
    get_mer.wait()
    mer = jnp.concatenate(split2(mer_buf[...]), axis=1)
    mer = jnp.concatenate([mer, mer], axis=0)

    for g in range(count):
        for j in range(4):
            load(g, j).wait()
    for g in range(count):
        for q in range(2):
            t = jnp.dot(zon, buf[g, 192 * q : 192 * q + 192], preferred_element_type=jnp.float32)
            hi, lo = split2(t[:64] + t[64:])
            for i in range(4):
                put = pl.ds(pl.multiple_of(16 * ((4 * q + i + 4 * at_x + at_z) & 7), 16), 16)
                rows = slice(16 * i, 16 * i + 16)
                for j in range(4):
                    lanes = slice(j * ROWS, (j + 1) * ROWS)
                    mid[j, g, put, :ROWS] = hi[rows, lanes]
                    mid[j, g, put, ROWS:] = lo[rows, lanes]
    for j in range(4):
        v = jnp.dot(mid[j].reshape(count * 128, 2 * ROWS), mer, preferred_element_type=jnp.float32)
        for g in range(count):
            u = v[128 * g : 128 * g + 128]
            u = u[:, 128:] + u[:, :128]
            u = u.T.reshape(16, 8, 128)
            lanes = slice(128 * g, 128 * g + 128)
            if along_y:
                stage[j, :, :, lanes] = u
                continue
            for r in range(16):
                stage[j, 4 * (at_z ^ (r % 4)) + (at_x ^ (r // 4)), :, lanes] = u[r]
        store(j).start()
    for j in range(4):
        store(j).wait()


def restrict(x, mer, zon, first, count, along_y):
    lanes = count * 128
    return pl.pallas_call(
        functools.partial(restrict_kernel, first, count, along_y),
        out_shape=[jax.ShapeDtypeStruct((16, 8, lanes), jnp.float32)] * 4,
        in_specs=[ANY] * 3,
        out_specs=[ANY] * 4,
        scratch_shapes=[
            pltpu.VMEM((count, ROWS, 4 * ROWS), jnp.bfloat16),
            pltpu.VMEM((4, count, 128, 2 * ROWS), jnp.bfloat16),
            pltpu.VMEM(mer.shape, jnp.float32),
            pltpu.VMEM(zon.shape, jnp.float32),
            pltpu.VMEM((4, 16, 8, lanes), jnp.float32),
            pltpu.SemaphoreType.DMA((count, 4)),
            pltpu.SemaphoreType.DMA((2,)),
            pltpu.SemaphoreType.DMA((4,)),
        ],
        compiler_params=pltpu.CompilerParams(vmem_limit_bytes=56 * 2**20),
        cost_estimate=pl.CostEstimate(
            flops=count * 800_000_000, bytes_accessed=count * ROWS * ROWS * 16, transcendentals=0
        ),
        name=f"restrict_{first}",
    )(x, mer, zon)


def deal_kernel(p0, p1, p2, p3, near, far, stage, in_sems, out_sems):
    first = lax.axis_index("y") ^ own_member()
    loads = [pltpu.make_async_copy(p, stage.at[k], in_sems.at[k]) for k, p in enumerate((p0, p1, p2, p3))]
    for c in loads:
        c.start()
    for c in loads:
        c.wait()
    for case in range(4):

        @pl.when(first == case)
        def _():
            stores = []
            for k in range(4):
                zlo, core = divmod(case ^ k, 2)
                stores.append(pltpu.make_async_copy(stage.at[k], (near, far)[zlo].at[core], out_sems.at[k]))
            for c in stores:
                c.start()
            for c in stores:
                c.wait()


def deal(parts):
    shape = parts[0].shape
    return pl.pallas_call(
        deal_kernel,
        out_shape=[jax.ShapeDtypeStruct((2, *shape), jnp.float32)] * 2,
        in_specs=[ANY] * 4,
        out_specs=[ANY] * 2,
        scratch_shapes=[
            pltpu.VMEM((4, *shape), jnp.float32),
            pltpu.SemaphoreType.DMA((4,)),
            pltpu.SemaphoreType.DMA((4,)),
        ],
        cost_estimate=pl.CostEstimate(flops=0, bytes_accessed=32 * math.prod(shape), transcendentals=0),
        name="deal",
    )(*parts)


def swap_groups(v):
    group = lax.shift_right_logical(lax.broadcasted_iota(jnp.int32, (8, 128), 1), 4)
    for d in (1, 2, 4):
        moved = (group & d) != 0
        v = [jnp.where(moved, v[(i + d) & 7], v[i]) for i in range(8)]
    return [v[0]] + [pltpu.roll(v[8 - m], 128 - 16 * m, 1) for m in range(1, 8)]


def finish_kernel(levels, tiles1, tiles2, *refs):
    r1, refs = refs[:2], refs[2:]
    r2, out, b1, b2, stage, in_sems, r2_sems, out_sems = refs
    y, me = lax.axis_index("y"), own_member()

    loads = [pltpu.make_async_copy(r1[k], b1.at[k], in_sems.at[k]) for k in range(2)]
    own = 4 * lax.axis_index("x") + lax.axis_index("zhi")

    def load(h, k):
        rows = pl.ds(8 * h, 8)
        return pltpu.make_async_copy(r2.at[k, rows], b2.at[k, rows], r2_sems.at[h, k])

    def store(h, n):
        lanes = pl.ds(128 * h, 128)
        return pltpu.make_async_copy(stage.at[n, :, :, lanes], out.at[levels[n], :, :, lanes], out_sems.at[h, n])

    for c in loads:
        c.start()
    for h in range(2):
        for k in range(4):
            load(h, k).start()
    for c in loads:
        c.wait()
    scale = 1.0 / math.sqrt(M - 1)
    for h in range(2):
        lanes = slice(128 * h, 128 * h + 128)

        def shuffle(k, sums):
            sums = list(sums)
            load(h, k).wait()
            for tile in (*tiles1, *tiles2):
                if tile < CUT:
                    at = 128 * tile
                    p = me ^ k
                    v = [b1[k & 1, own ^ (8 * h + i), k >> 1, :, at : at + 128] for i in range(8)]
                else:
                    at = 128 * (tile - CUT)
                    p = y ^ k
                    v = [b2[k, 8 * h + i, :, at : at + 128] for i in range(8)]
                v = swap_groups(v)
                for i in range(8):
                    level, m = divmod(8 * tile + i, 20)
                    if level in levels:
                        n = level - levels[0]
                        stage[n, p * 20 + m, :, lanes] = v[i]
                        sums[n] = sums[n] + v[i]
            return tuple(sums)

        zero = jnp.zeros((8, 128), jnp.float32)
        sums = lax.fori_loop(0, 4, shuffle, (zero,) * len(levels))
        for n in range(len(levels)):
            mean = sums[n] / M

            def centre(q, _):
                for m in range(20):
                    stage[n, q * 20 + m, :, lanes] = (stage[n, q * 20 + m, :, lanes] - mean) * scale
                return 0

            lax.fori_loop(0, 4, centre, 0)
            store(h, n).start()
    for h in range(2):
        for n in range(len(levels)):
            store(h, n).wait()


def finish(r1, r2):
    levels, tiles1, tiles2 = (0, 1, 2, 3), tuple(range(CUT)), tuple(range(CUT, GROUPS))
    return pl.pallas_call(
        functools.partial(finish_kernel, levels, tiles1, tiles2),
        out_shape=jax.ShapeDtypeStruct((4, M, 8, 256), jnp.float32),
        in_specs=[ANY] * 3,
        out_specs=ANY,
        scratch_shapes=[
            pltpu.VMEM((2, 16, 2, 8, 128 * len(tiles1)), jnp.float32),
            pltpu.VMEM((4, 16, 8, 128 * len(tiles2)), jnp.float32),
            pltpu.VMEM((len(levels), M, 8, 256), jnp.float32),
            pltpu.SemaphoreType.DMA((2,)),
            pltpu.SemaphoreType.DMA((2, 4)),
            pltpu.SemaphoreType.DMA((2, len(levels))),
        ],
        compiler_params=pltpu.CompilerParams(vmem_limit_bytes=16 * 2**20),
        cost_estimate=pl.CostEstimate(
            flops=len(levels) * 2_000_000, bytes_accessed=len(levels) * 1_300_000, transcendentals=0
        ),
        name="finish",
    )(*r1, r2)


def swap(unit, k):
    return [(d, d ^ (unit * k)) for d in range(256)]


def along(unit, parts):
    return [parts[0]] + [lax.ppermute(parts[k], AX, swap(unit, k)) for k in (1, 2, 3)]


def regroup_kernel(*refs):
    parts, outs = refs[:4], refs[4:]
    for i in range(4):
        for k in range(4):
            outs[k][i] = parts[i][:, k]


def regroup(parts):
    lanes = parts[0].shape[-1]
    parts = [p.reshape(4, 4, 8, lanes) for p in parts]
    vmem = pl.BlockSpec(memory_space=pltpu.VMEM)
    return pl.pallas_call(
        regroup_kernel,
        out_shape=[jax.ShapeDtypeStruct((4, 4, 8, lanes), jnp.float32)] * 4,
        in_specs=[vmem] * 4,
        out_specs=[vmem] * 4,
        cost_estimate=pl.CostEstimate(flops=500_000_000_000, bytes_accessed=800_000_000, transcendentals=0),
        name="regroup",
    )(*parts)


def planes():
    return [[(y ^ j) * 64 + y * 16 + b for j in range(4) for b in range(16)] for y in range(4)]


def body(member_predictions, meridional_operator, zonal_operator):
    x = member_predictions.reshape(-1, member_predictions.shape[-1])
    ops = (meridional_operator, zonal_operator)
    one = restrict(x, *ops, 0, CUT, False)
    x, *one = lax.optimization_barrier((x, *one))
    one = along(16, one)
    two = restrict(x, *ops, CUT, GROUPS - CUT, True)
    merged = lax.optimization_barrier((*one, *two))
    one, two = merged[:4], merged[4:]
    near, far = [p.reshape(2, 4, 4, 8, -1) for p in deal(one)]
    far = lax.ppermute(far, AX, swap(128, 1))
    one = along(1, [jnp.stack([near[:, k], far[:, k]], axis=0) for k in range(4)])
    two = jnp.concatenate(along(16, two), axis=0)
    two = lax.all_to_all(two, AX, 0, 0, axis_index_groups=planes(), tiled=True).reshape(4, 16, 8, -1)
    one = along(4, regroup(one))
    one = [p.reshape(4, 2, 2, 8, -1) for p in one]
    stay, leave = [jnp.concatenate([p[:, :, k] for p in one], axis=0) for k in range(2)]
    one = [stay, lax.ppermute(leave, AX, swap(64, 1))]
    return finish(one, two)


def solution(mesh):
    fine = Mesh(mesh.devices.reshape(2, 2, 4, 4, 4), AX)
    member, tile = ("zlo", "core"), ("y", "x", "zhi")
    in_specs = (P(None, member, tile, None), P(), P(tile, None))
    out_specs = P(None, None, tile, member)
    return jax.shard_map(body, mesh=fine, in_specs=in_specs, out_specs=out_specs, check_vma=False)
```

time: 117 us -> 110 us (0.940)
  waiting for transfers between devices: 65.6 us -> 46.4 us
  starting transfers between devices: 26.8 us -> 35.4 us
  local copies, waits for them, and re-layouts: 0.02 us -> 4.75 us
    all_to_all x2 -> x1, waiting for transfers between devices: 42.7 us -> 2.05 us  [body(): lax.all_to_all(two, AX, 0, 0, axis_index_groups=planes(), tiled=True)]
    ppermute x6 -> x14, waiting for transfers between devices: 22.9 us -> 44.4 us  [the longest x12 36.3 us: along(): lax.ppermute(parts[k], AX, swap(unit, k))]
    ppermute x6 -> x14, starting transfers between devices: 9.56 us -> 22.9 us  [the longest x12 22.7 us: along(): lax.ppermute(parts[k], AX, swap(unit, k))]
    all_to_all x2 -> x1, starting transfers between devices: 17.2 us -> 12.5 us  [body(): lax.all_to_all(two, AX, 0, 0, axis_index_groups=planes(), tiled=True)]
    pallas_call x2 -> x1, Pallas kernels: 6.5 us -> 3.71 us  [finish(): pl.pallas_call(functools.partial(finish_kernel, levels, tiles1, tiles2),...]
    pallas_call x2 -> x4, Pallas kernels: 15.1 us -> 16.9 us  [the longest x2 12.5 us: restrict(): pl.pallas_call(functools.partial(restrict_kernel, first, count, along_y),...]
    unnamed x10 -> x20, local copies, waits for them, and re-layouts: 0.02 us -> 1.45 us
    another operation x0 -> x2, local copies, waits for them, and re-layouts: none -> 1.17 us  [body(): jnp.stack([near[:, k], far[:, k]], axis=0)]
  transfers between devices with their start and end apart: 8 -> 15, of which waited for: 7 -> 11; matrix products, arithmetic and copies ran while one was open for 1% -> 4% of each run, Pallas kernels for 10% -> 8%
where the time goes in v2:
time: 110 us; the launch traced here: 109 us
  waiting for transfers between devices  46.4 us (42%)
  starting transfers between devices  35.4 us (32%)
  Pallas kernels  20.6 us (19%)
  local copies, waits for them, and re-layouts  4.75 us (4%)
  other arithmetic  2.12 us (2%)
    ppermute x12, waiting for transfers between devices, along(): lax.ppermute(parts[k], AX, swap(unit, k))  36.3 us
    ppermute x12, starting transfers between devices, along(): lax.ppermute(parts[k], AX, swap(unit, k))  22.7 us
    pallas_call x2, Pallas kernels, restrict(): pl.pallas_call(functools.partial(restrict_kernel, first, count, along_y),...  12.5 us
    all_to_all x1, starting transfers between devices, body(): lax.all_to_all(two, AX, 0, 0, axis_index_groups=planes(), tiled=True)  12.5 us
    ppermute x1, waiting for transfers between devices, body(): far = lax.ppermute(far, AX, swap(128, 1))  6.23 us
    pallas_call x1, Pallas kernels, finish(): pl.pallas_call(functools.partial(finish_kernel, levels, tiles1, tiles2),...  3.71 us
    pallas_call x1, Pallas kernels, deal(): pl.pallas_call(deal_kernel, out_shape=[jax.ShapeDtypeStruct((2, *shape),...  2.21 us
  transfers between devices with their start and end apart: 15, of which 11 were waited for; matrix products, arithmetic and copies ran while one was open for 4% of the time, Pallas kernels for 8%

profile of v2, /device:TPU:32, one launch (start us, length us, event | category | flops | bytes accessed | tf_op | source)
XLA Modules:
  0.0 109.5 jit_solution(6454810642879110908)
XLA Ops:
  0.0 5.4 %restrict_0.1 = (f32[16,8,512]{2,1,0:T(8,128)}, f32[16,8,512]{2,1,0:T(8,128)}, f32[16,8,512]{2,1,0:T(8,128)}, f32[16,8,512]{2,1,0:T(8,128)}) custom-call(bf16[3840,1536]{1,0:T(8,128)(2,1)} %bitcast.68, f32[384,128]{1,0:T(8,128)} %mer_ref.3, f32[16,48]{1,0:T(8,128)} %zon_ref.3), custom_call_target="tpu_custom_call" | custom-call | flops 3200000000 | bytes 9437184 | tf_op jit(solution)/shard_map/restrict_0/pallas_call | solution.py:100
  5.4 1.7 %collective-permute-start = (f32[16,8,512]{2,1,0:T(8,128)}, f32[16,8,512]{2,1,0:T(8,128)S(1)}, u32[]{:S(2)}, u32[]{:S(2)}) collective-permute-start(f32[16,8,512]{2,1,0:T(8,128)} %get-tuple-element.37), channel_id=1, source_target_pairs={{0,16},{1,17},{2,18},{3,19},{4,20},{5,21},{6,22},{7,23},{8,24},{9,... | collective-permute-start | bytes 786440 | tf_op jit(solution)/shard_map/ppermute | solution.py:262
  7.0 2.9 %collective-permute-start.1 = (f32[16,8,512]{2,1,0:T(8,128)}, f32[16,8,512]{2,1,0:T(8,128)S(1)}, u32[]{:S(2)}, u32[]{:S(2)}) collective-permute-start(f32[16,8,512]{2,1,0:T(8,128)} %get-tuple-element.38), channel_id=1, source_target_pairs={{0,32},{1,33},{2,34},{3,35},{4,36},{5,37},{6,38},{7,39},{8,40},{9,... | collective-permute-start | bytes 786440 | tf_op jit(solution)/shard_map/ppermute | solution.py:262
  10.2 7.1 %restrict_4.1 = (f32[16,8,768]{2,1,0:T(8,128)}, f32[16,8,768]{2,1,0:T(8,128)}, f32[16,8,768]{2,1,0:T(8,128)}, f32[16,8,768]{2,1,0:T(8,128)}) custom-call(bf16[3840,1536]{1,0:T(8,128)(2,1)} %bitcast.69, f32[384,128]{1,0:T(8,128)} %mer_ref.3, f32[16,48]{1,0:T(8,128)} %zon_ref.3), custom_call_target="tpu_custom_call" | custom-call | flops 4800000000 | bytes 14155776 | tf_op jit(solution)/shard_map/restrict_4/pallas_call | solution.py:100
  17.3 4.6 %collective-permute-done.1.p2 = f32[16,8,512]{2,1,0:T(8,128)S(1)} collective-permute-done((f32[16,8,512]{2,1,0:T(8,128)}, f32[16,8,512]{2,1,0:T(8,128)S(1)}, u32[]{:S(2)}, u32[]{:S(2)}) %collective-permute-start.1) | collective-permute-done | bytes 262176 | tf_op jit(solution)/shard_map/ppermute | solution.py:262
  21.9 2.6 %collective-permute-done.2.p3 = f32[16,8,512]{2,1,0:T(8,128)S(1)} collective-permute-done((f32[16,8,512]{2,1,0:T(8,128)}, f32[16,8,512]{2,1,0:T(8,128)S(1)}, u32[]{:S(2)}, u32[]{:S(2)}) %collective-permute-start.2) | collective-permute-done | bytes 262176 | tf_op jit(solution)/shard_map/ppermute | solution.py:262
  24.5 0.7 copy-done.3
  25.2 2.2 %deal.1 = (f32[2,16,8,512]{3,2,1,0:T(8,128)}, f32[2,16,8,512]{3,2,1,0:T(8,128)}) custom-call(f32[16,8,512]{2,1,0:T(8,128)} %get-tuple-element.45.p0, f32[16,8,512]{2,1,0:T(8,128)} %copy-done.1, f32[16,8,512]{2,1,0:T(8,128)} %copy-done.2, f32[16,8,512]{2,1,0:T(8,128)} %copy-done.3), custom_call_target="tpu_custom_call" | custom-call | bytes 2097152 | tf_op jit(solution)/shard_map/deal/pallas_call | solution.py:146
  27.4 1.1 copy.10
  28.7 1.7 %collective-permute-start.12 = (f32[16,8,768]{2,1,0:T(8,128)S(1)}, f32[16,8,768]{2,1,0:T(8,128)S(1)}, u32[]{:S(2)}, u32[]{:S(2)}) collective-permute-start(f32[16,8,768]{2,1,0:T(8,128)S(1)} %copy-done.5), channel_id=1, source_target_pairs={{0,32},{1,33},{2,34},{3,35},{4,36},{5,37},{6,38},{7,39},{8,40},{9,... | collective-permute-start | bytes 1179656 | tf_op jit(solution)/shard_map/ppermute | solution.py:262
  30.4 3.0 %collective-permute-start.13 = (f32[16,8,768]{2,1,0:T(8,128)S(1)}, f32[16,8,768]{2,1,0:T(8,128)S(1)}, u32[]{:S(2)}, u32[]{:S(2)}) collective-permute-start(f32[16,8,768]{2,1,0:T(8,128)S(1)} %copy-done.4), channel_id=1, source_target_pairs={{0,48},{1,49},{2,50},{3,51},{4,52},{5,53},{6,54},{7,55},{8,56},{9,... | collective-permute-start | bytes 1179656 | tf_op jit(solution)/shard_map/ppermute | solution.py:262
  33.4 1.1 %slice_bitcast_fusion.9 = (f32[1,2,4,8,512]{4,3,2,1,0:T(8,128)S(1)}, f32[1,2,4,8,512]{4,3,2,1,0:T(8,128)S(1)}, f32[1,2,4,8,512]{4,3,2,1,0:T(8,128)S(1)}, f32[1,2,4,8,512]{4,3,2,1,0:T(8,128)S(1)}) fusion(f32[2,4,4,8,512]{4,3,2,1,0:T(8,128)} %bitcast.70), kind=kLoop, calls=%fused_computation.16 | loop fusion | bytes 1048576 | tf_op jit(solution)/shard_map/stack;squeeze | solution.py:301
  34.6 6.2 %collective-permute-done.3 = f32[2,4,4,8,512]{4,3,2,0,1:T(8,128)S(1)} collective-permute-done((f32[2,4,4,8,512]{4,3,2,0,1:T(8,128)S(1)}, f32[2,4,4,8,512]{4,3,2,0,1:T(8,128)S(1)}, u32[]{:S(2)}, u32[]{:S(2)}) %collective-permute-start.3) | collective-permute-done | bytes 524320 | tf_op jit(solution)/shard_map/ppermute | solution.py:300
  40.9 3.3 %collective-permute-start.4 = (f32[2,2,4,8,512]{4,3,2,1,0:T(8,128)S(1)}, f32[2,2,4,8,512]{4,3,2,1,0:T(8,128)S(1)}, u32[]{:S(2)}, u32[]{:S(2)}) collective-permute-start(f32[2,2,4,8,512]{4,3,2,1,0:T(8,128)S(1)} %pad_maximum_fusion.4), channel_id=1, source_target_pairs={{0,1},{1,0},{2,3},{3,2},{4,5},{5,4},{6,7},{7,6},{8,9},{9,8},{10,11... | collective-permute-start | bytes 786440 | tf_op jit(solution)/shard_map/ppermute | solution.py:262
  44.2 4.6 %collective-permute-start.5 = (f32[2,2,4,8,512]{4,3,2,1,0:T(8,128)S(1)}, f32[2,2,4,8,512]{4,3,2,1,0:T(8,128)S(1)}, u32[]{:S(2)}, u32[]{:S(2)}) collective-permute-start(f32[2,2,4,8,512]{4,3,2,1,0:T(8,128)S(1)} %pad_maximum_fusion.5), channel_id=1, source_target_pairs={{0,2},{1,3},{2,0},{3,1},{4,6},{5,7},{6,4},{7,5},{8,10},{9,11},{10,... | collective-permute-start | bytes 786440 | tf_op jit(solution)/shard_map/ppermute | solution.py:262
  49.0 1.2 %pad_maximum_fusion = f32[64,8,768]{2,1,0:T(8,128)} fusion(f32[16,8,768]{2,1,0:T(8,128)S(1)} %collective-permute-done.13, f32[16,8,768]{2,1,0:T(8,128)S(1)} %collective-permute-done.12, f32[16,8,768]{2,1,0:T(8,128)S(1)} %collective-permute-done.11, f32[16,8,768]{2,1,0:T(8,128)S(1)} %copy-done), kind=kLoop, calls=%fused_computation | loop fusion | flops 1179648 | bytes 3145728 | tf_op jit(solution)/shard_map/concatenate | solution.py:302
  50.2 12.5 %all-to-all-start = ((f32[64,8,768]{2,1,0:T(8,128)}), f32[64,8,768]{2,1,0:T(8,128)}, u32[]{:S(2)}, u32[]{:S(2)}) async-start(f32[64,8,768]{2,1,0:T(8,128)} %pad_maximum_fusion), calls=%async_computation | async-start | bytes 3145728 | tf_op jit(solution)/shard_map/all_to_all | solution.py:303
  62.7 0.7 pad_maximum_fusion.3
  63.4 1.6 %collective-permute-done.4 = f32[2,2,4,8,512]{4,3,2,1,0:T(8,128)S(1)} collective-permute-done((f32[2,2,4,8,512]{4,3,2,1,0:T(8,128)S(1)}, f32[2,2,4,8,512]{4,3,2,1,0:T(8,128)S(1)}, u32[]{:S(2)}, u32[]{:S(2)}) %collective-permute-start.4) | collective-permute-done | bytes 262176 | tf_op jit(solution)/shard_map/ppermute | solution.py:262
  65.1 2.7 %collective-permute-done.5 = f32[2,2,4,8,512]{4,3,2,1,0:T(8,128)S(1)} collective-permute-done((f32[2,2,4,8,512]{4,3,2,1,0:T(8,128)S(1)}, f32[2,2,4,8,512]{4,3,2,1,0:T(8,128)S(1)}, u32[]{:S(2)}, u32[]{:S(2)}) %collective-permute-start.5) | collective-permute-done | bytes 262176 | tf_op jit(solution)/shard_map/ppermute | solution.py:262
  67.8 10.9 %collective-permute-done.6 = f32[2,2,4,8,512]{4,3,2,1,0:T(8,128)S(1)} collective-permute-done((f32[2,2,4,8,512]{4,3,2,1,0:T(8,128)S(1)}, f32[2,2,4,8,512]{4,3,2,1,0:T(8,128)S(1)}, u32[]{:S(2)}, u32[]{:S(2)}) %collective-permute-start.6) | collective-permute-done | bytes 262176 | tf_op jit(solution)/shard_map/ppermute | solution.py:262
  78.7 0.7 copy-done.9
  79.4 2.2 %regroup.1 = (f32[4,4,8,512]{3,2,1,0:T(8,128)}, f32[4,4,8,512]{3,2,1,0:T(8,128)}, f32[4,4,8,512]{3,2,1,0:T(8,128)}, f32[4,4,8,512]{3,2,1,0:T(8,128)}) custom-call(f32[4,4,8,512]{3,2,1,0:T(8,128)} %bitcast.74, f32[4,4,8,512]{3,2,1,0:T(8,128)} %bitcast.77, f32[4,4,8,512]{3,2,1,0:T(8,128)} %bitcast.78, f32[4,4,8,512]{3,2,1,0:T(8,128)} %bitcast.79), custom_call_target="tpu_custom_call" | custom-call | flops 499999997952 | bytes 800000000 | tf_op jit(solution)/shard_map/regroup/pallas_call | solution.py:276
  81.6 1.7 %collective-permute-start.7 = (f32[4,4,8,512]{3,2,1,0:T(8,128)}, f32[4,4,8,512]{3,2,1,0:T(8,128)S(1)}, u32[]{:S(2)}, u32[]{:S(2)}) collective-permute-start(f32[4,4,8,512]{3,2,1,0:T(8,128)} %get-tuple-element.52), channel_id=1, source_target_pairs={{0,4},{1,5},{2,6},{3,7},{4,0},{5,1},{6,2},{7,3},{8,12},{9,13},{10,... | collective-permute-start | bytes 786440 | tf_op jit(solution)/shard_map/ppermute | solution.py:262
  83.3 3.3 %collective-permute-start.8 = (f32[4,4,8,512]{3,2,1,0:T(8,128)}, f32[4,4,8,512]{3,2,1,0:T(8,128)S(1)}, u32[]{:S(2)}, u32[]{:S(2)}) collective-permute-start(f32[4,4,8,512]{3,2,1,0:T(8,128)} %get-tuple-element.53), channel_id=1, source_target_pairs={{0,8},{1,9},{2,10},{3,11},{4,12},{5,13},{6,14},{7,15},{8,0},{9,1},... | collective-permute-start | bytes 786440 | tf_op jit(solution)/shard_map/ppermute | solution.py:262
  86.6 1.0 slice_bitcast_fusion.3
  87.7 3.6 %collective-permute-done.7 = f32[4,4,8,512]{3,2,1,0:T(8,128)S(1)} collective-permute-done((f32[4,4,8,512]{3,2,1,0:T(8,128)}, f32[4,4,8,512]{3,2,1,0:T(8,128)S(1)}, u32[]{:S(2)}, u32[]{:S(2)}) %collective-permute-start.7) | collective-permute-done | bytes 262176 | tf_op jit(solution)/shard_map/ppermute | solution.py:262
  91.4 7.3 %collective-permute-done.8 = f32[4,4,8,512]{3,2,1,0:T(8,128)S(1)} collective-permute-done((f32[4,4,8,512]{3,2,1,0:T(8,128)}, f32[4,4,8,512]{3,2,1,0:T(8,128)S(1)}, u32[]{:S(2)}, u32[]{:S(2)}) %collective-permute-start.8) | collective-permute-done | bytes 262176 | tf_op jit(solution)/shard_map/ppermute | solution.py:262
  98.7 3.0 %collective-permute-done.9 = f32[4,4,8,512]{3,2,1,0:T(8,128)S(1)} collective-permute-done((f32[4,4,8,512]{3,2,1,0:T(8,128)}, f32[4,4,8,512]{3,2,1,0:T(8,128)S(1)}, u32[]{:S(2)}, u32[]{:S(2)}) %collective-permute-start.9) | collective-permute-done | bytes 262176 | tf_op jit(solution)/shard_map/ppermute | solution.py:262
  101.9 1.9 %collective-permute-done.10.refs_1_ = f32[16,2,8,512]{3,2,1,0:T(8,128)S(1)} collective-permute-done((f32[16,2,8,512]{3,2,1,0:T(8,128)S(1)}, f32[16,2,8,512]{3,2,1,0:T(8,128)S(1)}, u32[]{:S(2)}, u32[]{:S(2)}) %collective-permute-start.10) | collective-permute-done | bytes 524320 | tf_op jit(solution)/shard_map/ppermute | solution.py:307
  103.7 2.0 %all-to-all-done = f32[64,8,768]{2,1,0:T(8,128)} async-done(((f32[64,8,768]{2,1,0:T(8,128)}), f32[64,8,768]{2,1,0:T(8,128)}, u32[]{:S(2)}, u32[]{:S(2)}) %all-to-all-start) | async-done | bytes 1572896 | tf_op jit(solution)/shard_map/all_to_all | solution.py:303
  105.8 3.7 %finish.1 = f32[4,80,8,256]{3,2,1,0:T(8,128)} custom-call(f32[16,2,8,512]{3,2,1,0:T(8,128)S(1)} %pad_maximum_fusion.1.refs_0_, f32[16,2,8,512]{3,2,1,0:T(8,128)S(1)} %collective-permute-done.10.refs_1_, f32[4,16,8,768]{3,2,1,0:T(8,128)} %bitcast.27.refs_2_), custom_call_target="tpu_custom_call" | custom-call | flops 8000000 | bytes 5200000 | tf_op jit(solution)/shard_map/finish/pallas_call | solution.py:236
  (37 shorter events, 1.0 us)
Async XLA Ops:
  5.4 11.9 %collective-permute-start = (f32[16,8,512]{2,1,0:T(8,128)}, f32[16,8,512]{2,1,0:T(8,128)S(1)}, u32[]{:S(2)}, u32[]{:S(2)}) collective-permute-start(f32[16,8,512]{2,1,0:T(8,128)} %get-tuple-element.37), channel_id=1, source_target_pairs={{0,16},{1,17},{2,18},{3,19},{4,20},{5,21},{6,22},{7,23},{8,24},{9,... | collective-permute-start | bytes 786440 | tf_op jit(solution)/shard_map/ppermute | solution.py:262
  7.0 14.9 %collective-permute-start.1 = (f32[16,8,512]{2,1,0:T(8,128)}, f32[16,8,512]{2,1,0:T(8,128)S(1)}, u32[]{:S(2)}, u32[]{:S(2)}) collective-permute-start(f32[16,8,512]{2,1,0:T(8,128)} %get-tuple-element.38), channel_id=1, source_target_pairs={{0,32},{1,33},{2,34},{3,35},{4,36},{5,37},{6,38},{7,39},{8,40},{9,... | collective-permute-start | bytes 786440 | tf_op jit(solution)/shard_map/ppermute | solution.py:262
  9.9 14.5 %collective-permute-start.2 = (f32[16,8,512]{2,1,0:T(8,128)}, f32[16,8,512]{2,1,0:T(8,128)S(1)}, u32[]{:S(2)}, u32[]{:S(2)}) collective-permute-start(f32[16,8,512]{2,1,0:T(8,128)} %get-tuple-element.39), channel_id=1, source_target_pairs={{0,48},{1,49},{2,50},{3,51},{4,52},{5,53},{6,54},{7,55},{8,56},{9,... | collective-permute-start | bytes 786440 | tf_op jit(solution)/shard_map/ppermute | solution.py:262
  17.3 11.4 %copy-start.6 = (f32[16,8,768]{2,1,0:T(8,128)S(1)}, f32[16,8,768]{2,1,0:T(8,128)}, u32[]{:S(2)}) copy-start(f32[16,8,768]{2,1,0:T(8,128)} %get-tuple-element.56) | copy-start | bytes 1179652
  17.3 11.4 %copy-start.5 = (f32[16,8,768]{2,1,0:T(8,128)S(1)}, f32[16,8,768]{2,1,0:T(8,128)}, u32[]{:S(2)}) copy-start(f32[16,8,768]{2,1,0:T(8,128)} %get-tuple-element.57) | copy-start | bytes 1179652
  17.3 13.1 %copy-start.4 = (f32[16,8,768]{2,1,0:T(8,128)S(1)}, f32[16,8,768]{2,1,0:T(8,128)}, u32[]{:S(2)}) copy-start(f32[16,8,768]{2,1,0:T(8,128)} %get-tuple-element.58) | copy-start | bytes 1179652
  17.3 7.2 %copy-start.1 = (f32[16,8,512]{2,1,0:T(8,128)}, f32[16,8,512]{2,1,0:T(8,128)S(1)}, u32[]{:S(2)}) copy-start(f32[16,8,512]{2,1,0:T(8,128)S(1)} %collective-permute-done.p1) | copy-start | bytes 786436
  21.9 2.6 %copy-start.2 = (f32[16,8,512]{2,1,0:T(8,128)}, f32[16,8,512]{2,1,0:T(8,128)S(1)}, u32[]{:S(2)}) copy-start(f32[16,8,512]{2,1,0:T(8,128)S(1)} %collective-permute-done.1.p2) | copy-start | bytes 786436
  24.5 0.7 copy-start.3
  28.5 12.3 %collective-permute-start.3 = (f32[2,4,4,8,512]{4,3,2,0,1:T(8,128)S(1)}, f32[2,4,4,8,512]{4,3,2,0,1:T(8,128)S(1)}, u32[]{:S(2)}, u32[]{:S(2)}) collective-permute-start(f32[2,4,4,8,512]{4,3,2,0,1:T(8,128)S(1)} %copy.10), channel_id=1, source_target_pairs={{0,128},{1,129},{2,130},{3,131},{4,132},{5,133},{6,134},{7,135},{8... | collective-permute-start | bytes 1572872 | tf_op jit(solution)/shard_map/ppermute | solution.py:300
  28.7 20.1 %collective-permute-start.11 = (f32[16,8,768]{2,1,0:T(8,128)S(1)}, f32[16,8,768]{2,1,0:T(8,128)S(1)}, u32[]{:S(2)}, u32[]{:S(2)}) collective-permute-start(f32[16,8,768]{2,1,0:T(8,128)S(1)} %copy-done.6), channel_id=1, source_target_pairs={{0,16},{1,17},{2,18},{3,19},{4,20},{5,21},{6,22},{7,23},{8,24},{9,... | collective-permute-start | bytes 1179656 | tf_op jit(solution)/shard_map/ppermute | solution.py:262
  28.7 20.2 %collective-permute-start.12 = (f32[16,8,768]{2,1,0:T(8,128)S(1)}, f32[16,8,768]{2,1,0:T(8,128)S(1)}, u32[]{:S(2)}, u32[]{:S(2)}) collective-permute-start(f32[16,8,768]{2,1,0:T(8,128)S(1)} %copy-done.5), channel_id=1, source_target_pairs={{0,32},{1,33},{2,34},{3,35},{4,36},{5,37},{6,38},{7,39},{8,40},{9,... | collective-permute-start | bytes 1179656 | tf_op jit(solution)/shard_map/ppermute | solution.py:262
  30.4 18.5 %collective-permute-start.13 = (f32[16,8,768]{2,1,0:T(8,128)S(1)}, f32[16,8,768]{2,1,0:T(8,128)S(1)}, u32[]{:S(2)}, u32[]{:S(2)}) collective-permute-start(f32[16,8,768]{2,1,0:T(8,128)S(1)} %copy-done.4), channel_id=1, source_target_pairs={{0,48},{1,49},{2,50},{3,51},{4,52},{5,53},{6,54},{7,55},{8,56},{9,... | collective-permute-start | bytes 1179656 | tf_op jit(solution)/shard_map/ppermute | solution.py:262
  34.6 14.4 %copy-start = (f32[16,8,768]{2,1,0:T(8,128)S(1)}, f32[16,8,768]{2,1,0:T(8,128)}, u32[]{:S(2)}) copy-start(f32[16,8,768]{2,1,0:T(8,128)} %get-tuple-element.55) | copy-start | bytes 1179652
  40.9 24.2 %collective-permute-start.4 = (f32[2,2,4,8,512]{4,3,2,1,0:T(8,128)S(1)}, f32[2,2,4,8,512]{4,3,2,1,0:T(8,128)S(1)}, u32[]{:S(2)}, u32[]{:S(2)}) collective-permute-start(f32[2,2,4,8,512]{4,3,2,1,0:T(8,128)S(1)} %pad_maximum_fusion.4), channel_id=1, source_target_pairs={{0,1},{1,0},{2,3},{3,2},{4,5},{5,4},{6,7},{7,6},{8,9},{9,8},{10,11... | collective-permute-start | bytes 786440 | tf_op jit(solution)/shard_map/ppermute | solution.py:262
  44.2 23.6 %collective-permute-start.5 = (f32[2,2,4,8,512]{4,3,2,1,0:T(8,128)S(1)}, f32[2,2,4,8,512]{4,3,2,1,0:T(8,128)S(1)}, u32[]{:S(2)}, u32[]{:S(2)}) collective-permute-start(f32[2,2,4,8,512]{4,3,2,1,0:T(8,128)S(1)} %pad_maximum_fusion.5), channel_id=1, source_target_pairs={{0,2},{1,3},{2,0},{3,1},{4,6},{5,7},{6,4},{7,5},{8,10},{9,11},{10,... | collective-permute-start | bytes 786440 | tf_op jit(solution)/shard_map/ppermute | solution.py:262
  48.8 29.8 %collective-permute-start.6 = (f32[2,2,4,8,512]{4,3,2,1,0:T(8,128)S(1)}, f32[2,2,4,8,512]{4,3,2,1,0:T(8,128)S(1)}, u32[]{:S(2)}, u32[]{:S(2)}) collective-permute-start(f32[2,2,4,8,512]{4,3,2,1,0:T(8,128)S(1)} %pad_maximum_fusion.6), channel_id=1, source_target_pairs={{0,3},{1,2},{2,1},{3,0},{4,7},{5,6},{6,5},{7,4},{8,11},{9,10},{10,... | collective-permute-start | bytes 786440 | tf_op jit(solution)/shard_map/ppermute | solution.py:262
  50.2 55.5 %all-to-all-start = ((f32[64,8,768]{2,1,0:T(8,128)}), f32[64,8,768]{2,1,0:T(8,128)}, u32[]{:S(2)}, u32[]{:S(2)}) async-start(f32[64,8,768]{2,1,0:T(8,128)} %pad_maximum_fusion), calls=%async_computation | async-start | bytes 3145728 | tf_op jit(solution)/shard_map/all_to_all | solution.py:303
  65.1 13.6 %copy-start.7 = (f32[2,2,4,8,512]{4,3,2,1,0:T(8,128)}, f32[2,2,4,8,512]{4,3,2,1,0:T(8,128)S(1)}, u32[]{:S(2)}) copy-start(f32[2,2,4,8,512]{4,3,2,1,0:T(8,128)S(1)} %collective-permute-done.4) | copy-start | bytes 786436
  67.8 10.9 %copy-start.8 = (f32[2,2,4,8,512]{4,3,2,1,0:T(8,128)}, f32[2,2,4,8,512]{4,3,2,1,0:T(8,128)S(1)}, u32[]{:S(2)}) copy-start(f32[2,2,4,8,512]{4,3,2,1,0:T(8,128)S(1)} %collective-permute-done.5) | copy-start | bytes 786436
  78.7 0.7 copy-start.9
  81.6 9.8 %collective-permute-start.7 = (f32[4,4,8,512]{3,2,1,0:T(8,128)}, f32[4,4,8,512]{3,2,1,0:T(8,128)S(1)}, u32[]{:S(2)}, u32[]{:S(2)}) collective-permute-start(f32[4,4,8,512]{3,2,1,0:T(8,128)} %get-tuple-element.52), channel_id=1, source_target_pairs={{0,4},{1,5},{2,6},{3,7},{4,0},{5,1},{6,2},{7,3},{8,12},{9,13},{10,... | collective-permute-start | bytes 786440 | tf_op jit(solution)/shard_map/ppermute | solution.py:262
  83.3 15.3 %collective-permute-start.8 = (f32[4,4,8,512]{3,2,1,0:T(8,128)}, f32[4,4,8,512]{3,2,1,0:T(8,128)S(1)}, u32[]{:S(2)}, u32[]{:S(2)}) collective-permute-start(f32[4,4,8,512]{3,2,1,0:T(8,128)} %get-tuple-element.53), channel_id=1, source_target_pairs={{0,8},{1,9},{2,10},{3,11},{4,12},{5,13},{6,14},{7,15},{8,0},{9,1},... | collective-permute-start | bytes 786440 | tf_op jit(solution)/shard_map/ppermute | solution.py:262
  87.6 14.0 %collective-permute-start.9 = (f32[4,4,8,512]{3,2,1,0:T(8,128)}, f32[4,4,8,512]{3,2,1,0:T(8,128)S(1)}, u32[]{:S(2)}, u32[]{:S(2)}) collective-permute-start(f32[4,4,8,512]{3,2,1,0:T(8,128)} %get-tuple-element.54), channel_id=1, source_target_pairs={{0,12},{1,13},{2,14},{3,15},{4,8},{5,9},{6,10},{7,11},{8,4},{9,5},... | collective-permute-start | bytes 786440 | tf_op jit(solution)/shard_map/ppermute | solution.py:262
  101.7 2.0 %collective-permute-start.10 = (f32[16,2,8,512]{3,2,1,0:T(8,128)S(1)}, f32[16,2,8,512]{3,2,1,0:T(8,128)S(1)}, u32[]{:S(2)}, u32[]{:S(2)}) collective-permute-start(f32[16,2,8,512]{3,2,1,0:T(8,128)S(1)} %pad_maximum_fusion.2), channel_id=1, source_target_pairs={{0,64},{1,65},{2,66},{3,67},{4,68},{5,69},{6,70},{7,71},{8,72},{9,... | collective-permute-start | bytes 1572872 | tf_op jit(solution)/shard_map/ppermute | solution.py:307

commit v3 on v2

--- a/solution.py
+++ b/solution.py
@@ -31,11 +31,8 @@
     base = lax.axis_index("y")
     at_x, at_z = lax.axis_index("x"), lax.axis_index("zhi")
 
-    def load(g, j):
-        rows = pl.ds((first + g) * ROWS, ROWS)
-        lane = pl.multiple_of((base ^ j) * ROWS, 128)
-        to = buf.at[g, :, pl.ds(j * ROWS, ROWS)]
-        return pltpu.make_async_copy(x_ref.at[rows, pl.ds(lane, ROWS)], to, in_sems.at[g, j])
+    def load(g):
+        return pltpu.make_async_copy(x_ref.at[pl.ds((first + g) * ROWS, ROWS)], buf.at[g], in_sems.at[g])
 
     def store(j):
         return pltpu.make_async_copy(stage.at[j], outs[j], out_sems.at[j])
@@ -45,8 +42,7 @@
     get_zon.start()
     get_mer.start()
     for g in range(count):
-        for j in range(4):
-            load(g, j).start()
+        load(g).start()
     k = lax.broadcasted_iota(jnp.int32, (48, 192), 0)
     n = lax.broadcasted_iota(jnp.int32, (48, 192), 1)
     spread = jnp.where(lax.rem(n, 48) == k, 1.0, 0.0).astype(jnp.bfloat16)
@@ -65,8 +61,7 @@
     mer = jnp.concatenate([mer, mer], axis=0)
 
     for g in range(count):
-        for j in range(4):
-            load(g, j).wait()
+        load(g).wait()
     for g in range(count):
         for q in range(2):
             t = jnp.dot(zon, buf[g, 192 * q : 192 * q + 192], preferred_element_type=jnp.float32)
@@ -74,10 +69,10 @@
             for i in range(4):
                 put = pl.ds(pl.multiple_of(16 * ((4 * q + i + 4 * at_x + at_z) & 7), 16), 16)
                 rows = slice(16 * i, 16 * i + 16)
-                for j in range(4):
-                    lanes = slice(j * ROWS, (j + 1) * ROWS)
-                    mid[j, g, put, :ROWS] = hi[rows, lanes]
-                    mid[j, g, put, ROWS:] = lo[rows, lanes]
+                for b in range(4):
+                    lanes = slice(b * ROWS, (b + 1) * ROWS)
+                    mid[base ^ b, g, put, :ROWS] = hi[rows, lanes]
+                    mid[base ^ b, g, put, ROWS:] = lo[rows, lanes]
     for j in range(4):
         v = jnp.dot(mid[j].reshape(count * 128, 2 * ROWS), mer, preferred_element_type=jnp.float32)
         for g in range(count):
@@ -108,7 +103,7 @@
             pltpu.VMEM(mer.shape, jnp.float32),
             pltpu.VMEM(zon.shape, jnp.float32),
             pltpu.VMEM((4, 16, 8, lanes), jnp.float32),
-            pltpu.SemaphoreType.DMA((count, 4)),
+            pltpu.SemaphoreType.DMA((count,)),
             pltpu.SemaphoreType.DMA((2,)),
             pltpu.SemaphoreType.DMA((4,)),
         ],
@@ -120,7 +115,8 @@
     )(x, mer, zon)
 
 
-def deal_kernel(p0, p1, p2, p3, near, far, stage, in_sems, out_sems):
+def deal_kernel(p0, p1, p2, p3, *rest):
+    outs, (stage, in_sems, out_sems) = rest[:8], rest[8:]
     first = lax.axis_index("y") ^ own_member()
     loads = [pltpu.make_async_copy(p, stage.at[k], in_sems.at[k]) for k, p in enumerate((p0, p1, p2, p3))]
     for c in loads:
@@ -134,7 +130,9 @@
             stores = []
             for k in range(4):
                 zlo, core = divmod(case ^ k, 2)
-                stores.append(pltpu.make_async_copy(stage.at[k], (near, far)[zlo].at[core], out_sems.at[k]))
+                for z in range(4):
+                    to = outs[2 * z + zlo].at[core]
+                    stores.append(pltpu.make_async_copy(stage.at[k, pl.ds(4 * z, 4)], to, out_sems.at[k, z]))
             for c in stores:
                 c.start()
             for c in stores:
@@ -145,13 +143,13 @@
     shape = parts[0].shape
     return pl.pallas_call(
         deal_kernel,
-        out_shape=[jax.ShapeDtypeStruct((2, *shape), jnp.float32)] * 2,
+        out_shape=[jax.ShapeDtypeStruct((2, 4, *shape[1:]), jnp.float32)] * 8,
         in_specs=[ANY] * 4,
-        out_specs=[ANY] * 2,
+        out_specs=[ANY] * 8,
         scratch_shapes=[
             pltpu.VMEM((4, *shape), jnp.float32),
             pltpu.SemaphoreType.DMA((4,)),
-            pltpu.SemaphoreType.DMA((4,)),
+            pltpu.SemaphoreType.DMA((4, 4)),
         ],
         cost_estimate=pl.CostEstimate(flops=0, bytes_accessed=32 * math.prod(shape), transcendentals=0),
         name="deal",
@@ -259,24 +257,27 @@
 
 
 def along(unit, parts):
-    return [parts[0]] + [lax.ppermute(parts[k], AX, swap(unit, k)) for k in (1, 2, 3)]
+    got = {k: lax.ppermute(parts[k], AX, swap(unit, k)) for k in (2, 1, 3)}
+    return [parts[0], got[1], got[2], got[3]]
+
+
+Z_ORDER = (0, 1, 2, 6, 7, 3, 5, 4)
 
 
 def regroup_kernel(*refs):
-    parts, outs = refs[:4], refs[4:]
-    for i in range(4):
+    parts, outs = refs[:8], refs[8:]
+    for i, part in zip(Z_ORDER, parts):
         for k in range(4):
-            outs[k][i] = parts[i][:, k]
+            outs[k][i] = part[:, k]
 
 
 def regroup(parts):
     lanes = parts[0].shape[-1]
-    parts = [p.reshape(4, 4, 8, lanes) for p in parts]
     vmem = pl.BlockSpec(memory_space=pltpu.VMEM)
     return pl.pallas_call(
         regroup_kernel,
-        out_shape=[jax.ShapeDtypeStruct((4, 4, 8, lanes), jnp.float32)] * 4,
-        in_specs=[vmem] * 4,
+        out_shape=[jax.ShapeDtypeStruct((8, 2, 8, lanes), jnp.float32)] * 4,
+        in_specs=[vmem] * 8,
         out_specs=[vmem] * 4,
         cost_estimate=pl.CostEstimate(flops=500_000_000_000, bytes_accessed=800_000_000, transcendentals=0),
         name="regroup",
@@ -292,18 +293,13 @@
     ops = (meridional_operator, zonal_operator)
     one = restrict(x, *ops, 0, CUT, False)
     x, *one = lax.optimization_barrier((x, *one))
-    one = along(16, one)
+    one = deal(along(16, one))
+    one = [one[i] if i == 0 else lax.ppermute(one[i], AX, swap(1, 128 * (i & 1) + (i >> 1))) for i in Z_ORDER]
     two = restrict(x, *ops, CUT, GROUPS - CUT, True)
-    merged = lax.optimization_barrier((*one, *two))
-    one, two = merged[:4], merged[4:]
-    near, far = [p.reshape(2, 4, 4, 8, -1) for p in deal(one)]
-    far = lax.ppermute(far, AX, swap(128, 1))
-    one = along(1, [jnp.stack([near[:, k], far[:, k]], axis=0) for k in range(4)])
     two = jnp.concatenate(along(16, two), axis=0)
     two = lax.all_to_all(two, AX, 0, 0, axis_index_groups=planes(), tiled=True).reshape(4, 16, 8, -1)
     one = along(4, regroup(one))
-    one = [p.reshape(4, 2, 2, 8, -1) for p in one]
-    stay, leave = [jnp.concatenate([p[:, :, k] for p in one], axis=0) for k in range(2)]
+    stay, leave = [jnp.concatenate([p[:, k] for p in one], axis=0).reshape(16, 2, 8, -1) for k in range(2)]
     one = [stay, lax.ppermute(leave, AX, swap(64, 1))]
     return finish(one, two)
 

time: 110 us -> 104 us (0.945)
  waiting for transfers between devices: 46.4 us -> 34.7 us
  starting transfers between devices: 35.4 us -> 41.4 us
    ppermute x13 -> x16, waiting for transfers between devices: 42.5 us -> 24.8 us  [the longest x9 21.6 us: along(): got = {k: lax.ppermute(parts[k], AX, swap(unit, k)) for k in (2, 1, 3)}]
    ppermute x13 -> x16, starting transfers between devices: 22.8 us -> 32 us  [the longest x7 18 us: body(): lax.ppermute(one[i], AX, swap(1, 128 * (i & 1) + (i >> 1)))]
    all_to_all x1, waiting for transfers between devices: 2.05 us -> 8.06 us  [body(): lax.all_to_all(two, AX, 0, 0, axis_index_groups=planes(), tiled=True)]
    all_to_all x1, starting transfers between devices: 12.5 us -> 9.18 us  [body(): lax.all_to_all(two, AX, 0, 0, axis_index_groups=planes(), tiled=True)]
    pallas_call x0 -> x2, local copies, waits for them, and re-layouts: none -> 1.98 us  [regroup(): pl.pallas_call(regroup_kernel, out_shape=[jax.ShapeDtypeStruct((8, 2, 8,...]
    another operation x2 -> x0, local copies, waits for them, and re-layouts: 1.17 us -> none  [body(): jnp.stack([near[:, k], far[:, k]], axis=0)]
  transfers between devices with their start and end apart: 15 -> 18, of which waited for: 11 -> 8; matrix products, arithmetic and copies ran while one was open for 4% -> 5% of each run, Pallas kernels for 8% -> 11%
where the time goes in v3:
time: 104 us
  starting transfers between devices  41.4 us (40%)
  waiting for transfers between devices  34.7 us (33%)
  Pallas kernels  20.8 us (20%)
  local copies, waits for them, and re-layouts  4.43 us (4%)
  other arithmetic  2.31 us (2%)
    ppermute x9, waiting for transfers between devices, along(): got = {k: lax.ppermute(parts[k], AX, swap(unit, k)) for k in (2, 1, 3)}  21.6 us
    ppermute x7, starting transfers between devices, body(): lax.ppermute(one[i], AX, swap(1, 128 * (i & 1) + (i >> 1)))  18 us
    ppermute x9, starting transfers between devices, along(): got = {k: lax.ppermute(parts[k], AX, swap(unit, k)) for k in (2, 1, 3)}  14 us
    pallas_call x2, Pallas kernels, restrict(): pl.pallas_call(functools.partial(restrict_kernel, first, count, along_y),...  12.4 us
    all_to_all x1, starting transfers between devices, body(): lax.all_to_all(two, AX, 0, 0, axis_index_groups=planes(), tiled=True)  9.18 us
    all_to_all x1, waiting for transfers between devices, body(): lax.all_to_all(two, AX, 0, 0, axis_index_groups=planes(), tiled=True)  8.06 us
    pallas_call x1, Pallas kernels, finish(): pl.pallas_call(functools.partial(finish_kernel, levels, tiles1, tiles2),...  3.71 us
    ppermute x7, waiting for transfers between devices, body(): lax.ppermute(one[i], AX, swap(1, 128 * (i & 1) + (i >> 1)))  3.27 us
  transfers between devices with their start and end apart: 18, of which 8 were waited for; matrix products, arithmetic and copies ran while one was open for 5% of the time, Pallas kernels for 11%

profile of v3, /device:TPU:32, one launch (start us, length us, event | category | flops | bytes accessed | tf_op | source)
XLA Modules:
  0.0 103.9 jit_solution(6773043247081971611)
XLA Ops:
  0.0 5.4 %restrict_0.1 = (f32[16,8,512]{2,1,0:T(8,128)}, f32[16,8,512]{2,1,0:T(8,128)}, f32[16,8,512]{2,1,0:T(8,128)}, f32[16,8,512]{2,1,0:T(8,128)}) custom-call(bf16[3840,1536]{1,0:T(8,128)(2,1)} %bitcast.23, f32[384,128]{1,0:T(8,128)} %mer_ref.3, f32[16,48]{1,0:T(8,128)} %zon_ref.3), custom_call_target="tpu_custom_call" | custom-call | flops 3200000000 | bytes 9437184 | tf_op jit(solution)/shard_map/restrict_0/pallas_call | solution.py:95
  5.4 1.7 %collective-permute-start = (f32[16,8,512]{2,1,0:T(8,128)}, f32[16,8,512]{2,1,0:T(8,128)S(1)}, u32[]{:S(2)}, u32[]{:S(2)}) collective-permute-start(f32[16,8,512]{2,1,0:T(8,128)} %get-tuple-element.35), channel_id=1, source_target_pairs={{0,16},{1,17},{2,18},{3,19},{4,20},{5,21},{6,22},{7,23},{8,24},{9,... | collective-permute-start | bytes 786440 | tf_op jit(solution)/shard_map/ppermute | solution.py:260
  7.0 2.9 %collective-permute-start.1 = (f32[16,8,512]{2,1,0:T(8,128)}, f32[16,8,512]{2,1,0:T(8,128)S(1)}, u32[]{:S(2)}, u32[]{:S(2)}) collective-permute-start(f32[16,8,512]{2,1,0:T(8,128)} %get-tuple-element.36), channel_id=1, source_target_pairs={{0,32},{1,33},{2,34},{3,35},{4,36},{5,37},{6,38},{7,39},{8,40},{9,... | collective-permute-start | bytes 786440 | tf_op jit(solution)/shard_map/ppermute | solution.py:260
  10.2 7.1 %restrict_4.1 = (f32[16,8,768]{2,1,0:T(8,128)}, f32[16,8,768]{2,1,0:T(8,128)}, f32[16,8,768]{2,1,0:T(8,128)}, f32[16,8,768]{2,1,0:T(8,128)}) custom-call(bf16[3840,1536]{1,0:T(8,128)(2,1)} %bitcast.24, f32[384,128]{1,0:T(8,128)} %mer_ref.3, f32[16,48]{1,0:T(8,128)} %zon_ref.3), custom_call_target="tpu_custom_call" | custom-call | flops 4800000000 | bytes 14155776 | tf_op jit(solution)/shard_map/restrict_4/pallas_call | solution.py:95
  17.2 0.4 collective-permute-start.14
  17.7 4.1 %collective-permute-start.15 = (f32[16,8,768]{2,1,0:T(8,128)}, f32[16,8,768]{2,1,0:T(8,128)S(1)}, u32[]{:S(2)}, u32[]{:S(2)}) collective-permute-start(f32[16,8,768]{2,1,0:T(8,128)} %get-tuple-element.53), channel_id=1, source_target_pairs={{0,32},{1,33},{2,34},{3,35},{4,36},{5,37},{6,38},{7,39},{8,40},{9,... | collective-permute-start | bytes 1179656 | tf_op jit(solution)/shard_map/ppermute | solution.py:260
  22.0 2.6 %collective-permute-done.2.p3 = f32[16,8,512]{2,1,0:T(8,128)S(1)} collective-permute-done((f32[16,8,512]{2,1,0:T(8,128)}, f32[16,8,512]{2,1,0:T(8,128)S(1)}, u32[]{:S(2)}, u32[]{:S(2)}) %collective-permute-start.2) | collective-permute-done | bytes 262176 | tf_op jit(solution)/shard_map/ppermute | solution.py:260
  24.6 0.7 copy-done.2
  25.3 2.4 %deal.1 = (f32[2,4,8,512]{3,2,1,0:T(8,128)}, f32[2,4,8,512]{3,2,1,0:T(8,128)}, f32[2,4,8,512]{3,2,1,0:T(8,128)}, f32[2,4,8,512]{3,2,1,0:T(8,128)}, f32[2,4,8,512...) custom-call(f32[16,8,512]{2,1,0:T(8,128)} %get-tuple-element.34.p0, ...), custom_call_target="tpu_custom_call" | custom-call | bytes 2097152 | tf_op jit(solution)/shard_map/deal/pallas_call | solution.py:144
  27.9 3.3 %collective-permute-start.4 = (f32[2,4,8,512]{3,2,1,0:T(8,128)}, f32[2,4,8,512]{3,2,1,0:T(8,128)S(1)}, u32[]{:S(2)}, u32[]{:S(2)}) collective-permute-start(f32[2,4,8,512]{3,2,1,0:T(8,128)} %get-tuple-element.40), channel_id=1, source_target_pairs={{0,1},{1,0},{2,3},{3,2},{4,5},{5,4},{6,7},{7,6},{8,9},{9,8},{10,11... | collective-permute-start | bytes 393224 | tf_op jit(solution)/shard_map/ppermute | solution.py:297
  31.2 3.0 %collective-permute-done.3.refs_1_ = f32[2,4,8,512]{3,2,1,0:T(8,128)S(1)} collective-permute-done((f32[2,4,8,512]{3,2,1,0:T(8,128)}, f32[2,4,8,512]{3,2,1,0:T(8,128)S(1)}, u32[]{:S(2)}, u32[]{:S(2)}) %collective-permute-start.3) | collective-permute-done | bytes 131104 | tf_op jit(solution)/shard_map/ppermute | solution.py:297
  34.2 6.0 %collective-permute-start.5 = (f32[2,4,8,512]{3,2,1,0:T(8,128)}, f32[2,4,8,512]{3,2,1,0:T(8,128)S(1)}, u32[]{:S(2)}, u32[]{:S(2)}) collective-permute-start(f32[2,4,8,512]{3,2,1,0:T(8,128)} %get-tuple-element.41), channel_id=1, source_target_pairs={{0,3},{1,2},{2,1},{3,0},{4,7},{5,6},{6,5},{7,4},{8,11},{9,10},{10,... | collective-permute-start | bytes 393224 | tf_op jit(solution)/shard_map/ppermute | solution.py:297
  40.2 0.7 collective-permute-start.6
  40.9 1.0 collective-permute-start.7
  41.9 2.9 %collective-permute-start.8 = (f32[2,4,8,512]{3,2,1,0:T(8,128)}, f32[2,4,8,512]{3,2,1,0:T(8,128)S(1)}, u32[]{:S(2)}, u32[]{:S(2)}) collective-permute-start(f32[2,4,8,512]{3,2,1,0:T(8,128)} %get-tuple-element.44), channel_id=1, source_target_pairs={{0,130},{1,131},{2,128},{3,129},{4,134},{5,135},{6,132},{7,133},{8... | collective-permute-start | bytes 393224 | tf_op jit(solution)/shard_map/ppermute | solution.py:297
  44.7 4.0 %collective-permute-start.9 = (f32[2,4,8,512]{3,2,1,0:T(8,128)}, f32[2,4,8,512]{3,2,1,0:T(8,128)S(1)}, u32[]{:S(2)}, u32[]{:S(2)}) collective-permute-start(f32[2,4,8,512]{3,2,1,0:T(8,128)} %get-tuple-element.45), channel_id=1, source_target_pairs={{0,2},{1,3},{2,0},{3,1},{4,6},{5,7},{6,4},{7,5},{8,10},{9,11},{10,... | collective-permute-start | bytes 393224 | tf_op jit(solution)/shard_map/ppermute | solution.py:297
  48.7 2.2 %pad_maximum_fusion = f32[64,8,768]{2,1,0:T(8,128)} fusion(f32[16,8,768]{2,1,0:T(8,128)S(1)} %collective-permute-done.16, f32[16,8,768]{2,1,0:T(8,128)S(1)} %collective-permute-done.15, f32[16,8,768]{2,1,0:T(8,128)S(1)} %collective-permute-done.14, f32[16,8,768]{2,1,0:T(8,128)} %get-tuple-element.51), kind=kLoop, calls=%fused_computation | loop fusion | flops 1179648 | bytes 3145728 | tf_op jit(solution)/shard_map/concatenate | solution.py:299
  51.0 9.2 %all-to-all-start = ((f32[64,8,768]{2,1,0:T(8,128)}), f32[64,8,768]{2,1,0:T(8,128)}, u32[]{:S(2)}, u32[]{:S(2)}) async-start(f32[64,8,768]{2,1,0:T(8,128)} %pad_maximum_fusion), calls=%async_computation | async-start | bytes 3145728 | tf_op jit(solution)/shard_map/all_to_all | solution.py:300
  60.5 0.3 copy-done.6
  61.2 2.3 %regroup.1 = (f32[8,2,8,512]{3,2,1,0:T(8,128)}, f32[8,2,8,512]{3,2,1,0:T(8,128)}, f32[8,2,8,512]{3,2,1,0:T(8,128)}, f32[8,2,8,512]{3,2,1,0:T(8,128)}) custom-call(f32[2,4,8,512]{3,2,1,0:T(8,128)} %get-tuple-element.38.refs_0_, f32[2,4,8,512]{3,2,1,0:T(8,128)} %copy-done.4, f32[2,4,8,512]{3,2,1,0:T(8,128)} %copy-done.5, f32[2,4,8,512]{3,2,1,0:T(8,128)} %copy-done.6, ...), custom_call_target="tpu_custom_call" | custom-call | flops 499999997952 | bytes 800000000 | tf_op jit(solution)/shard_map/regroup/pallas_call | solution.py:277
  63.5 1.0 copy.6
  64.5 3.1 %collective-permute-start.11 = (f32[8,2,8,512]{3,2,0,1:T(8,128)S(1)}, f32[8,2,8,512]{3,2,0,1:T(8,128)S(1)}, u32[]{:S(2)}, u32[]{:S(2)}) collective-permute-start(f32[8,2,8,512]{3,2,0,1:T(8,128)S(1)} %copy.6), channel_id=1, source_target_pairs={{0,8},{1,9},{2,10},{3,11},{4,12},{5,13},{6,14},{7,15},{8,0},{9,1},... | collective-permute-start | bytes 786440 | tf_op jit(solution)/shard_map/ppermute | solution.py:260
  67.6 1.0 copy.5
  68.6 0.7 collective-permute-start.10
  69.2 1.0 slice_bitcast_fusion.3
  70.2 0.7 collective-permute-start.12
  70.9 9.5 %collective-permute-done.11 = f32[8,2,8,512]{3,2,0,1:T(8,128)S(1)} collective-permute-done((f32[8,2,8,512]{3,2,0,1:T(8,128)S(1)}, f32[8,2,8,512]{3,2,0,1:T(8,128)S(1)}, u32[]{:S(2)}, u32[]{:S(2)}) %collective-permute-start.11) | collective-permute-done | bytes 262176 | tf_op jit(solution)/shard_map/ppermute | solution.py:260
  80.5 8.3 %collective-permute-done.10 = f32[8,2,8,512]{3,2,0,1:T(8,128)S(1)} collective-permute-done((f32[8,2,8,512]{3,2,0,1:T(8,128)S(1)}, f32[8,2,8,512]{3,2,0,1:T(8,128)S(1)}, u32[]{:S(2)}, u32[]{:S(2)}) %collective-permute-start.10) | collective-permute-done | bytes 262176 | tf_op jit(solution)/shard_map/ppermute | solution.py:260
  88.8 1.1 %collective-permute-done.12 = f32[8,2,8,512]{3,2,1,0:T(8,128)S(1)} collective-permute-done((f32[8,2,8,512]{3,2,1,0:T(8,128)S(1)}, f32[8,2,8,512]{3,2,1,0:T(8,128)S(1)}, u32[]{:S(2)}, u32[]{:S(2)}) %collective-permute-start.12) | collective-permute-done | bytes 262176 | tf_op jit(solution)/shard_map/ppermute | solution.py:260
  90.2 1.8 %collective-permute-done.13.refs_1_ = f32[16,2,8,512]{3,2,1,0:T(8,128)S(1)} collective-permute-done((f32[16,2,8,512]{3,2,1,0:T(8,128)S(1)}, f32[16,2,8,512]{3,2,1,0:T(8,128)S(1)}, u32[]{:S(2)}, u32[]{:S(2)}) %collective-permute-start.13) | collective-permute-done | bytes 524320 | tf_op jit(solution)/shard_map/ppermute | solution.py:303
  92.0 8.1 %all-to-all-done = f32[64,8,768]{2,1,0:T(8,128)} async-done(((f32[64,8,768]{2,1,0:T(8,128)}), f32[64,8,768]{2,1,0:T(8,128)}, u32[]{:S(2)}, u32[]{:S(2)}) %all-to-all-start) | async-done | bytes 1572896 | tf_op jit(solution)/shard_map/all_to_all | solution.py:300
  100.0 3.7 %finish.1 = f32[4,80,8,256]{3,2,1,0:T(8,128)} custom-call(f32[16,2,8,512]{3,2,1,0:T(8,128)S(1)} %bitcast.22, f32[16,2,8,512]{3,2,1,0:T(8,128)S(1)} %collective-permute-done.13.refs_1_, f32[4,16,8,768]{3,2,1,0:T(8,128)} %bitcast.11.refs_2_), custom_call_target="tpu_custom_call" | custom-call | flops 8000000 | bytes 5200000 | tf_op jit(solution)/shard_map/finish/pallas_call | solution.py:234
  (40 shorter events, 1.6 us)
Async XLA Ops:
  5.4 16.4 %collective-permute-start = (f32[16,8,512]{2,1,0:T(8,128)}, f32[16,8,512]{2,1,0:T(8,128)S(1)}, u32[]{:S(2)}, u32[]{:S(2)}) collective-permute-start(f32[16,8,512]{2,1,0:T(8,128)} %get-tuple-element.35), channel_id=1, source_target_pairs={{0,16},{1,17},{2,18},{3,19},{4,20},{5,21},{6,22},{7,23},{8,24},{9,... | collective-permute-start | bytes 786440 | tf_op jit(solution)/shard_map/ppermute | solution.py:260
  7.0 15.0 %collective-permute-start.1 = (f32[16,8,512]{2,1,0:T(8,128)}, f32[16,8,512]{2,1,0:T(8,128)S(1)}, u32[]{:S(2)}, u32[]{:S(2)}) collective-permute-start(f32[16,8,512]{2,1,0:T(8,128)} %get-tuple-element.36), channel_id=1, source_target_pairs={{0,32},{1,33},{2,34},{3,35},{4,36},{5,37},{6,38},{7,39},{8,40},{9,... | collective-permute-start | bytes 786440 | tf_op jit(solution)/shard_map/ppermute | solution.py:260
  9.9 14.7 %collective-permute-start.2 = (f32[16,8,512]{2,1,0:T(8,128)}, f32[16,8,512]{2,1,0:T(8,128)S(1)}, u32[]{:S(2)}, u32[]{:S(2)}) collective-permute-start(f32[16,8,512]{2,1,0:T(8,128)} %get-tuple-element.37), channel_id=1, source_target_pairs={{0,48},{1,49},{2,50},{3,51},{4,52},{5,53},{6,54},{7,55},{8,56},{9,... | collective-permute-start | bytes 786440 | tf_op jit(solution)/shard_map/ppermute | solution.py:260
  17.2 23.6 %collective-permute-start.14 = (f32[16,8,768]{2,1,0:T(8,128)}, f32[16,8,768]{2,1,0:T(8,128)S(1)}, u32[]{:S(2)}, u32[]{:S(2)}) collective-permute-start(f32[16,8,768]{2,1,0:T(8,128)} %get-tuple-element.52), channel_id=1, source_target_pairs={{0,16},{1,17},{2,18},{3,19},{4,20},{5,21},{6,22},{7,23},{8,24},{9,... | collective-permute-start | bytes 1179656 | tf_op jit(solution)/shard_map/ppermute | solution.py:260
  17.7 24.2 %collective-permute-start.15 = (f32[16,8,768]{2,1,0:T(8,128)}, f32[16,8,768]{2,1,0:T(8,128)S(1)}, u32[]{:S(2)}, u32[]{:S(2)}) collective-permute-start(f32[16,8,768]{2,1,0:T(8,128)} %get-tuple-element.53), channel_id=1, source_target_pairs={{0,32},{1,33},{2,34},{3,35},{4,36},{5,37},{6,38},{7,39},{8,40},{9,... | collective-permute-start | bytes 1179656 | tf_op jit(solution)/shard_map/ppermute | solution.py:260
  21.8 2.9 %copy-start = (f32[16,8,512]{2,1,0:T(8,128)}, f32[16,8,512]{2,1,0:T(8,128)S(1)}, u32[]{:S(2)}) copy-start(f32[16,8,512]{2,1,0:T(8,128)S(1)} %collective-permute-done.p1) | copy-start | bytes 786436
  21.8 23.0 %collective-permute-start.16 = (f32[16,8,768]{2,1,0:T(8,128)}, f32[16,8,768]{2,1,0:T(8,128)S(1)}, u32[]{:S(2)}, u32[]{:S(2)}) collective-permute-start(f32[16,8,768]{2,1,0:T(8,128)} %get-tuple-element.54), channel_id=1, source_target_pairs={{0,48},{1,49},{2,50},{3,51},{4,52},{5,53},{6,54},{7,55},{8,56},{9,... | collective-permute-start | bytes 1179656 | tf_op jit(solution)/shard_map/ppermute | solution.py:260
  22.0 2.6 %copy-start.1 = (f32[16,8,512]{2,1,0:T(8,128)}, f32[16,8,512]{2,1,0:T(8,128)S(1)}, u32[]{:S(2)}) copy-start(f32[16,8,512]{2,1,0:T(8,128)S(1)} %collective-permute-done.1.p2) | copy-start | bytes 786436
  24.6 0.7 copy-start.2
  27.7 6.5 %collective-permute-start.3 = (f32[2,4,8,512]{3,2,1,0:T(8,128)}, f32[2,4,8,512]{3,2,1,0:T(8,128)S(1)}, u32[]{:S(2)}, u32[]{:S(2)}) collective-permute-start(f32[2,4,8,512]{3,2,1,0:T(8,128)} %get-tuple-element.39), channel_id=1, source_target_pairs={{0,128},{1,129},{2,130},{3,131},{4,132},{5,133},{6,134},{7,135},{8... | collective-permute-start | bytes 393224 | tf_op jit(solution)/shard_map/ppermute | solution.py:297
  27.9 12.3 %collective-permute-start.4 = (f32[2,4,8,512]{3,2,1,0:T(8,128)}, f32[2,4,8,512]{3,2,1,0:T(8,128)S(1)}, u32[]{:S(2)}, u32[]{:S(2)}) collective-permute-start(f32[2,4,8,512]{3,2,1,0:T(8,128)} %get-tuple-element.40), channel_id=1, source_target_pairs={{0,1},{1,0},{2,3},{3,2},{4,5},{5,4},{6,7},{7,6},{8,9},{9,8},{10,11... | collective-permute-start | bytes 393224 | tf_op jit(solution)/shard_map/ppermute | solution.py:297
  34.2 16.8 %copy-start.4 = (f32[2,4,8,512]{3,2,1,0:T(8,128)}, f32[2,4,8,512]{3,2,1,0:T(8,128)S(1)}, u32[]{:S(2)}) copy-start(f32[2,4,8,512]{3,2,1,0:T(8,128)S(1)} %collective-permute-done.3.refs_1_) | copy-start | bytes 393220
  34.2 26.0 %collective-permute-start.5 = (f32[2,4,8,512]{3,2,1,0:T(8,128)}, f32[2,4,8,512]{3,2,1,0:T(8,128)S(1)}, u32[]{:S(2)}, u32[]{:S(2)}) collective-permute-start(f32[2,4,8,512]{3,2,1,0:T(8,128)} %get-tuple-element.41), channel_id=1, source_target_pairs={{0,3},{1,2},{2,1},{3,0},{4,7},{5,6},{6,5},{7,4},{8,11},{9,10},{10,... | collective-permute-start | bytes 393224 | tf_op jit(solution)/shard_map/ppermute | solution.py:297
  40.2 10.8 %copy-start.5 = (f32[2,4,8,512]{3,2,1,0:T(8,128)}, f32[2,4,8,512]{3,2,1,0:T(8,128)S(1)}, u32[]{:S(2)}) copy-start(f32[2,4,8,512]{3,2,1,0:T(8,128)S(1)} %collective-permute-done.4.refs_2_) | copy-start | bytes 393220
  40.2 20.0 %collective-permute-start.6 = (f32[2,4,8,512]{3,2,1,0:T(8,128)}, f32[2,4,8,512]{3,2,1,0:T(8,128)S(1)}, u32[]{:S(2)}, u32[]{:S(2)}) collective-permute-start(f32[2,4,8,512]{3,2,1,0:T(8,128)} %get-tuple-element.42), channel_id=1, source_target_pairs={{0,131},{1,130},{2,129},{3,128},{4,135},{5,134},{6,133},{7,132},{8... | collective-permute-start | bytes 393224 | tf_op jit(solution)/shard_map/ppermute | solution.py:297
  40.9 19.4 %collective-permute-start.7 = (f32[2,4,8,512]{3,2,1,0:T(8,128)}, f32[2,4,8,512]{3,2,1,0:T(8,128)S(1)}, u32[]{:S(2)}, u32[]{:S(2)}) collective-permute-start(f32[2,4,8,512]{3,2,1,0:T(8,128)} %get-tuple-element.43), channel_id=1, source_target_pairs={{0,129},{1,128},{2,131},{3,130},{4,133},{5,132},{6,135},{7,134},{8... | collective-permute-start | bytes 393224 | tf_op jit(solution)/shard_map/ppermute | solution.py:297
  41.9 18.6 %collective-permute-start.8 = (f32[2,4,8,512]{3,2,1,0:T(8,128)}, f32[2,4,8,512]{3,2,1,0:T(8,128)S(1)}, u32[]{:S(2)}, u32[]{:S(2)}) collective-permute-start(f32[2,4,8,512]{3,2,1,0:T(8,128)} %get-tuple-element.44), channel_id=1, source_target_pairs={{0,130},{1,131},{2,128},{3,129},{4,134},{5,135},{6,132},{7,133},{8... | collective-permute-start | bytes 393224 | tf_op jit(solution)/shard_map/ppermute | solution.py:297
  44.7 15.8 %collective-permute-start.9 = (f32[2,4,8,512]{3,2,1,0:T(8,128)}, f32[2,4,8,512]{3,2,1,0:T(8,128)S(1)}, u32[]{:S(2)}, u32[]{:S(2)}) collective-permute-start(f32[2,4,8,512]{3,2,1,0:T(8,128)} %get-tuple-element.45), channel_id=1, source_target_pairs={{0,2},{1,3},{2,0},{3,1},{4,6},{5,7},{6,4},{7,5},{8,10},{9,11},{10,... | collective-permute-start | bytes 393224 | tf_op jit(solution)/shard_map/ppermute | solution.py:297
  51.0 49.0 %all-to-all-start = ((f32[64,8,768]{2,1,0:T(8,128)}), f32[64,8,768]{2,1,0:T(8,128)}, u32[]{:S(2)}, u32[]{:S(2)}) async-start(f32[64,8,768]{2,1,0:T(8,128)} %pad_maximum_fusion), calls=%async_computation | async-start | bytes 3145728 | tf_op jit(solution)/shard_map/all_to_all | solution.py:300
  60.2 0.7 copy-start.6
  60.2 0.7 copy-start.7
  60.2 0.7 copy-start.8
  60.5 0.7 copy-start.9
  60.5 0.7 copy-start.10
  63.5 6.7 %copy-start.3 = (f32[8,2,8,512]{3,2,1,0:T(8,128)S(1)}, f32[8,2,8,512]{3,2,1,0:T(8,128)}, u32[]{:S(2)}) copy-start(f32[8,2,8,512]{3,2,1,0:T(8,128)} %get-tuple-element.49) | copy-start | bytes 786436
  64.5 15.9 %collective-permute-start.11 = (f32[8,2,8,512]{3,2,0,1:T(8,128)S(1)}, f32[8,2,8,512]{3,2,0,1:T(8,128)S(1)}, u32[]{:S(2)}, u32[]{:S(2)}) collective-permute-start(f32[8,2,8,512]{3,2,0,1:T(8,128)S(1)} %copy.6), channel_id=1, source_target_pairs={{0,8},{1,9},{2,10},{3,11},{4,12},{5,13},{6,14},{7,15},{8,0},{9,1},... | collective-permute-start | bytes 786440 | tf_op jit(solution)/shard_map/ppermute | solution.py:260
  68.6 20.2 %collective-permute-start.10 = (f32[8,2,8,512]{3,2,0,1:T(8,128)S(1)}, f32[8,2,8,512]{3,2,0,1:T(8,128)S(1)}, u32[]{:S(2)}, u32[]{:S(2)}) collective-permute-start(f32[8,2,8,512]{3,2,0,1:T(8,128)S(1)} %copy.5), channel_id=1, source_target_pairs={{0,4},{1,5},{2,6},{3,7},{4,0},{5,1},{6,2},{7,3},{8,12},{9,13},{10,... | collective-permute-start | bytes 786440 | tf_op jit(solution)/shard_map/ppermute | solution.py:260
  70.2 19.7 %collective-permute-start.12 = (f32[8,2,8,512]{3,2,1,0:T(8,128)S(1)}, f32[8,2,8,512]{3,2,1,0:T(8,128)S(1)}, u32[]{:S(2)}, u32[]{:S(2)}) collective-permute-start(f32[8,2,8,512]{3,2,1,0:T(8,128)S(1)} %copy-done.3), channel_id=1, source_target_pairs={{0,12},{1,13},{2,14},{3,15},{4,8},{5,9},{6,10},{7,11},{8,4},{9,5},... | collective-permute-start | bytes 786440 | tf_op jit(solution)/shard_map/ppermute | solution.py:260
  90.0 2.0 %collective-permute-start.13 = (f32[16,2,8,512]{3,2,1,0:T(8,128)S(1)}, f32[16,2,8,512]{3,2,1,0:T(8,128)S(1)}, u32[]{:S(2)}, u32[]{:S(2)}) collective-permute-start(f32[16,2,8,512]{3,2,1,0:T(8,128)S(1)} %bitcast.25), channel_id=1, source_target_pairs={{0,64},{1,65},{2,66},{3,67},{4,68},{5,69},{6,70},{7,71},{8,72},{9,... | collective-permute-start | bytes 1572872 | tf_op jit(solution)/shard_map/ppermute | solution.py:303

commit v4 on v3

--- a/solution.py
+++ b/solution.py
@@ -107,7 +107,7 @@
             pltpu.SemaphoreType.DMA((2,)),
             pltpu.SemaphoreType.DMA((4,)),
         ],
-        compiler_params=pltpu.CompilerParams(vmem_limit_bytes=56 * 2**20),
+        compiler_params=pltpu.CompilerParams(vmem_limit_bytes=(53 if along_y else 56) * 2**20),
         cost_estimate=pl.CostEstimate(
             flops=count * 800_000_000, bytes_accessed=count * ROWS * ROWS * 16, transcendentals=0
         ),

time: 104 us -> 103 us (level)
  waiting for transfers between devices: 34.7 us -> 33.4 us
  Pallas kernels: 20.8 us -> 21.9 us
    ppermute x9, waiting for transfers between devices: 21.6 us -> 19 us  [along(): got = {k: lax.ppermute(parts[k], AX, swap(unit, k)) for k in (2, 1, 3)}]
    ppermute x7, waiting for transfers between devices: 3.27 us -> 4.49 us  [body(): lax.ppermute(one[i], AX, swap(1, 128 * (i & 1) + (i >> 1)))]
    pallas_call x2, Pallas kernels: 12.4 us -> 13.5 us  [restrict(): pl.pallas_call(functools.partial(restrict_kernel, first, count, along_y),...]
  transfers between devices with their start and end apart: 18 -> 18, of which waited for: 8 -> 8; matrix products, arithmetic and copies ran while one was open for 5% -> 4% of each run, Pallas kernels for 11% -> 12%
where the time goes in v4:
time: 103 us
  starting transfers between devices  41.3 us (40%)
  waiting for transfers between devices  33.4 us (32%)
  Pallas kernels  21.9 us (21%)
  local copies, waits for them, and re-layouts  4.4 us (4%)
  other arithmetic  1.32 us (1%)
    ppermute x9, waiting for transfers between devices, along(): got = {k: lax.ppermute(parts[k], AX, swap(unit, k)) for k in (2, 1, 3)}  19 us
    ppermute x7, starting transfers between devices, body(): lax.ppermute(one[i], AX, swap(1, 128 * (i & 1) + (i >> 1)))  18.1 us
    ppermute x9, starting transfers between devices, along(): got = {k: lax.ppermute(parts[k], AX, swap(unit, k)) for k in (2, 1, 3)}  14 us
    pallas_call x2, Pallas kernels, restrict(): pl.pallas_call(functools.partial(restrict_kernel, first, count, along_y),...  13.5 us
    all_to_all x1, starting transfers between devices, body(): lax.all_to_all(two, AX, 0, 0, axis_index_groups=planes(), tiled=True)  9.01 us
    all_to_all x1, waiting for transfers between devices, body(): lax.all_to_all(two, AX, 0, 0, axis_index_groups=planes(), tiled=True)  8.13 us
    ppermute x7, waiting for transfers between devices, body(): lax.ppermute(one[i], AX, swap(1, 128 * (i & 1) + (i >> 1)))  4.49 us
    pallas_call x1, Pallas kernels, finish(): pl.pallas_call(functools.partial(finish_kernel, levels, tiles1, tiles2),...  3.71 us
  transfers between devices with their start and end apart: 18, of which 8 were waited for; matrix products, arithmetic and copies ran while one was open for 4% of the time, Pallas kernels for 12%

profile of v4, /device:TPU:32, one launch (start us, length us, event | category | flops | bytes accessed | tf_op | source)
XLA Modules:
  0.0 102.6 jit_solution(3145402790863159676)
XLA Ops:
  0.0 5.4 %restrict_0.1 = (f32[16,8,512]{2,1,0:T(8,128)}, f32[16,8,512]{2,1,0:T(8,128)}, f32[16,8,512]{2,1,0:T(8,128)}, f32[16,8,512]{2,1,0:T(8,128)}) custom-call(bf16[3840,1536]{1,0:T(8,128)(2,1)} %bitcast.23, f32[384,128]{1,0:T(8,128)} %mer_ref.3, f32[16,48]{1,0:T(8,128)} %zon_ref.3), custom_call_target="tpu_custom_call" | custom-call | flops 3200000000 | bytes 9437184 | tf_op jit(solution)/shard_map/restrict_0/pallas_call | solution.py:95
  5.4 1.7 %collective-permute-start = (f32[16,8,512]{2,1,0:T(8,128)}, f32[16,8,512]{2,1,0:T(8,128)S(1)}, u32[]{:S(2)}, u32[]{:S(2)}) collective-permute-start(f32[16,8,512]{2,1,0:T(8,128)} %get-tuple-element.35), channel_id=1, source_target_pairs={{0,16},{1,17},{2,18},{3,19},{4,20},{5,21},{6,22},{7,23},{8,24},{9,... | collective-permute-start | bytes 786440 | tf_op jit(solution)/shard_map/ppermute | solution.py:260
  7.1 2.9 %collective-permute-start.1 = (f32[16,8,512]{2,1,0:T(8,128)}, f32[16,8,512]{2,1,0:T(8,128)S(1)}, u32[]{:S(2)}, u32[]{:S(2)}) collective-permute-start(f32[16,8,512]{2,1,0:T(8,128)} %get-tuple-element.36), channel_id=1, source_target_pairs={{0,32},{1,33},{2,34},{3,35},{4,36},{5,37},{6,38},{7,39},{8,40},{9,... | collective-permute-start | bytes 786440 | tf_op jit(solution)/shard_map/ppermute | solution.py:260
  10.2 8.1 %restrict_4.1 = (f32[16,8,768]{2,1,0:T(8,128)S(1)}, f32[16,8,768]{2,1,0:T(8,128)}, f32[16,8,768]{2,1,0:T(8,128)}, f32[16,8,768]{2,1,0:T(8,128)}) custom-call(bf16[3840,1536]{1,0:T(8,128)(2,1)} %bitcast.24, f32[384,128]{1,0:T(8,128)S(1)} %copy-done, f32[16,48]{1,0:T(8,128)S(1)} %copy-done.1), custom_call_target="tpu_custom_call" | custom-call | flops 4800000000 | bytes 14155776 | tf_op jit(solution)/shard_map/restrict_4/pallas_call | solution.py:95
  18.8 4.1 %collective-permute-start.15 = (f32[16,8,768]{2,1,0:T(8,128)}, f32[16,8,768]{2,1,0:T(8,128)S(1)}, u32[]{:S(2)}, u32[]{:S(2)}) collective-permute-start(f32[16,8,768]{2,1,0:T(8,128)} %get-tuple-element.53), channel_id=1, source_target_pairs={{0,32},{1,33},{2,34},{3,35},{4,36},{5,37},{6,38},{7,39},{8,40},{9,... | collective-permute-start | bytes 1179656 | tf_op jit(solution)/shard_map/ppermute | solution.py:260
  23.1 1.4 %collective-permute-done.2.p3 = f32[16,8,512]{2,1,0:T(8,128)S(1)} collective-permute-done((f32[16,8,512]{2,1,0:T(8,128)}, f32[16,8,512]{2,1,0:T(8,128)S(1)}, u32[]{:S(2)}, u32[]{:S(2)}) %collective-permute-start.2) | collective-permute-done | bytes 262176 | tf_op jit(solution)/shard_map/ppermute | solution.py:260
  24.5 0.7 copy-done.4
  25.2 2.4 %deal.1 = (f32[2,4,8,512]{3,2,1,0:T(8,128)}, f32[2,4,8,512]{3,2,1,0:T(8,128)}, f32[2,4,8,512]{3,2,1,0:T(8,128)}, f32[2,4,8,512]{3,2,1,0:T(8,128)}, f32[2,4,8,512...) custom-call(f32[16,8,512]{2,1,0:T(8,128)} %get-tuple-element.34.p0, ...), custom_call_target="tpu_custom_call" | custom-call | bytes 2097152 | tf_op jit(solution)/shard_map/deal/pallas_call | solution.py:144
  27.6 1.2 %collective-permute-start.3 = (f32[2,4,8,512]{3,2,1,0:T(8,128)}, f32[2,4,8,512]{3,2,1,0:T(8,128)S(1)}, u32[]{:S(2)}, u32[]{:S(2)}) collective-permute-start(f32[2,4,8,512]{3,2,1,0:T(8,128)} %get-tuple-element.39), channel_id=1, source_target_pairs={{0,128},{1,129},{2,130},{3,131},{4,132},{5,133},{6,134},{7,135},{8... | collective-permute-start | bytes 393224 | tf_op jit(solution)/shard_map/ppermute | solution.py:297
  28.8 2.2 %collective-permute-start.4 = (f32[2,4,8,512]{3,2,1,0:T(8,128)}, f32[2,4,8,512]{3,2,1,0:T(8,128)S(1)}, u32[]{:S(2)}, u32[]{:S(2)}) collective-permute-start(f32[2,4,8,512]{3,2,1,0:T(8,128)} %get-tuple-element.40), channel_id=1, source_target_pairs={{0,1},{1,0},{2,3},{3,2},{4,5},{5,4},{6,7},{7,6},{8,9},{9,8},{10,11... | collective-permute-start | bytes 393224 | tf_op jit(solution)/shard_map/ppermute | solution.py:297
  31.0 2.9 %collective-permute-done.3.refs_1_ = f32[2,4,8,512]{3,2,1,0:T(8,128)S(1)} collective-permute-done((f32[2,4,8,512]{3,2,1,0:T(8,128)}, f32[2,4,8,512]{3,2,1,0:T(8,128)S(1)}, u32[]{:S(2)}, u32[]{:S(2)}) %collective-permute-start.3) | collective-permute-done | bytes 131104 | tf_op jit(solution)/shard_map/ppermute | solution.py:297
  33.9 6.1 %collective-permute-start.5 = (f32[2,4,8,512]{3,2,1,0:T(8,128)}, f32[2,4,8,512]{3,2,1,0:T(8,128)S(1)}, u32[]{:S(2)}, u32[]{:S(2)}) collective-permute-start(f32[2,4,8,512]{3,2,1,0:T(8,128)} %get-tuple-element.41), channel_id=1, source_target_pairs={{0,3},{1,2},{2,1},{3,0},{4,7},{5,6},{6,5},{7,4},{8,11},{9,10},{10,... | collective-permute-start | bytes 393224 | tf_op jit(solution)/shard_map/ppermute | solution.py:297
  40.1 0.8 collective-permute-start.6
  40.9 1.0 %collective-permute-start.7 = (f32[2,4,8,512]{3,2,1,0:T(8,128)}, f32[2,4,8,512]{3,2,1,0:T(8,128)S(1)}, u32[]{:S(2)}, u32[]{:S(2)}) collective-permute-start(f32[2,4,8,512]{3,2,1,0:T(8,128)} %get-tuple-element.43), channel_id=1, source_target_pairs={{0,129},{1,128},{2,131},{3,130},{4,133},{5,132},{6,135},{7,134},{8... | collective-permute-start | bytes 393224 | tf_op jit(solution)/shard_map/ppermute | solution.py:297
  41.9 3.6 %collective-permute-start.8 = (f32[2,4,8,512]{3,2,1,0:T(8,128)}, f32[2,4,8,512]{3,2,1,0:T(8,128)S(1)}, u32[]{:S(2)}, u32[]{:S(2)}) collective-permute-start(f32[2,4,8,512]{3,2,1,0:T(8,128)} %get-tuple-element.44), channel_id=1, source_target_pairs={{0,130},{1,131},{2,128},{3,129},{4,134},{5,135},{6,132},{7,133},{8... | collective-permute-start | bytes 393224 | tf_op jit(solution)/shard_map/ppermute | solution.py:297
  45.5 3.1 %collective-permute-start.9 = (f32[2,4,8,512]{3,2,1,0:T(8,128)}, f32[2,4,8,512]{3,2,1,0:T(8,128)S(1)}, u32[]{:S(2)}, u32[]{:S(2)}) collective-permute-start(f32[2,4,8,512]{3,2,1,0:T(8,128)} %get-tuple-element.45), channel_id=1, source_target_pairs={{0,2},{1,3},{2,0},{3,1},{4,6},{5,7},{6,4},{7,5},{8,10},{9,11},{10,... | collective-permute-start | bytes 393224 | tf_op jit(solution)/shard_map/ppermute | solution.py:297
  48.6 1.2 %pad_maximum_fusion = f32[64,8,768]{2,1,0:T(8,128)} fusion(f32[16,8,768]{2,1,0:T(8,128)S(1)} %collective-permute-done.16, f32[16,8,768]{2,1,0:T(8,128)S(1)} %collective-permute-done.15, f32[16,8,768]{2,1,0:T(8,128)S(1)} %collective-permute-done.14, f32[16,8,768]{2,1,0:T(8,128)S(1)} %get-tuple-element.51), kind=kLoop, calls=%fused_computation | loop fusion | flops 1179648 | bytes 3145728 | tf_op jit(solution)/shard_map/concatenate | solution.py:299
  49.9 9.0 %all-to-all-start = ((f32[64,8,768]{2,1,0:T(8,128)}), f32[64,8,768]{2,1,0:T(8,128)}, u32[]{:S(2)}, u32[]{:S(2)}) async-start(f32[64,8,768]{2,1,0:T(8,128)} %pad_maximum_fusion), calls=%async_computation | async-start | bytes 3145728 | tf_op jit(solution)/shard_map/all_to_all | solution.py:300
  58.9 1.6 %collective-permute-done.8.refs_6_ = f32[2,4,8,512]{3,2,1,0:T(8,128)S(1)} collective-permute-done((f32[2,4,8,512]{3,2,1,0:T(8,128)}, f32[2,4,8,512]{3,2,1,0:T(8,128)S(1)}, u32[]{:S(2)}, u32[]{:S(2)}) %collective-permute-start.8) | collective-permute-done | bytes 131104 | tf_op jit(solution)/shard_map/ppermute | solution.py:297
  61.2 2.3 %regroup.1 = (f32[8,2,8,512]{3,2,1,0:T(8,128)}, f32[8,2,8,512]{3,2,1,0:T(8,128)}, f32[8,2,8,512]{3,2,1,0:T(8,128)}, f32[8,2,8,512]{3,2,1,0:T(8,128)}) custom-call(f32[2,4,8,512]{3,2,1,0:T(8,128)} %get-tuple-element.38.refs_0_, f32[2,4,8,512]{3,2,1,0:T(8,128)} %copy-done.6, f32[2,4,8,512]{3,2,1,0:T(8,128)} %copy-done.7, f32[2,4,8,512]{3,2,1,0:T(8,128)} %copy-done.8, ...), custom_call_target="tpu_custom_call" | custom-call | flops 499999997952 | bytes 800000000 | tf_op jit(solution)/shard_map/regroup/pallas_call | solution.py:277
  63.5 1.0 copy.6
  64.5 3.1 %collective-permute-start.11 = (f32[8,2,8,512]{3,2,0,1:T(8,128)S(1)}, f32[8,2,8,512]{3,2,0,1:T(8,128)S(1)}, u32[]{:S(2)}, u32[]{:S(2)}) collective-permute-start(f32[8,2,8,512]{3,2,0,1:T(8,128)S(1)} %copy.6), channel_id=1, source_target_pairs={{0,8},{1,9},{2,10},{3,11},{4,12},{5,13},{6,14},{7,15},{8,0},{9,1},... | collective-permute-start | bytes 786440 | tf_op jit(solution)/shard_map/ppermute | solution.py:260
  67.6 1.0 copy.5
  68.6 0.7 collective-permute-start.10
  69.3 1.0 slice_bitcast_fusion.3
  70.3 0.7 collective-permute-start.12
  70.9 9.3 %collective-permute-done.11 = f32[8,2,8,512]{3,2,0,1:T(8,128)S(1)} collective-permute-done((f32[8,2,8,512]{3,2,0,1:T(8,128)S(1)}, f32[8,2,8,512]{3,2,0,1:T(8,128)S(1)}, u32[]{:S(2)}, u32[]{:S(2)}) %collective-permute-start.11) | collective-permute-done | bytes 262176 | tf_op jit(solution)/shard_map/ppermute | solution.py:260
  80.3 7.2 %collective-permute-done.10 = f32[8,2,8,512]{3,2,0,1:T(8,128)S(1)} collective-permute-done((f32[8,2,8,512]{3,2,0,1:T(8,128)S(1)}, f32[8,2,8,512]{3,2,0,1:T(8,128)S(1)}, u32[]{:S(2)}, u32[]{:S(2)}) %collective-permute-start.10) | collective-permute-done | bytes 262176 | tf_op jit(solution)/shard_map/ppermute | solution.py:260
  87.5 1.0 %collective-permute-done.12 = f32[8,2,8,512]{3,2,1,0:T(8,128)S(1)} collective-permute-done((f32[8,2,8,512]{3,2,1,0:T(8,128)S(1)}, f32[8,2,8,512]{3,2,1,0:T(8,128)S(1)}, u32[]{:S(2)}, u32[]{:S(2)}) %collective-permute-start.12) | collective-permute-done | bytes 262176 | tf_op jit(solution)/shard_map/ppermute | solution.py:260
  88.8 1.8 %collective-permute-done.13.refs_1_ = f32[16,2,8,512]{3,2,1,0:T(8,128)S(1)} collective-permute-done((f32[16,2,8,512]{3,2,1,0:T(8,128)S(1)}, f32[16,2,8,512]{3,2,1,0:T(8,128)S(1)}, u32[]{:S(2)}, u32[]{:S(2)}) %collective-permute-start.13) | collective-permute-done | bytes 524320 | tf_op jit(solution)/shard_map/ppermute | solution.py:303
  90.6 8.1 %all-to-all-done = f32[64,8,768]{2,1,0:T(8,128)} async-done(((f32[64,8,768]{2,1,0:T(8,128)}), f32[64,8,768]{2,1,0:T(8,128)}, u32[]{:S(2)}, u32[]{:S(2)}) %all-to-all-start) | async-done | bytes 1572896 | tf_op jit(solution)/shard_map/all_to_all | solution.py:300
  98.8 3.7 %finish.1 = f32[4,80,8,256]{3,2,1,0:T(8,128)} custom-call(f32[16,2,8,512]{3,2,1,0:T(8,128)S(1)} %bitcast.22, f32[16,2,8,512]{3,2,1,0:T(8,128)S(1)} %collective-permute-done.13.refs_1_, f32[4,16,8,768]{3,2,1,0:T(8,128)} %bitcast.11.refs_2_), custom_call_target="tpu_custom_call" | custom-call | flops 8000000 | bytes 5200000 | tf_op jit(solution)/shard_map/finish/pallas_call | solution.py:234
  (44 shorter events, 1.9 us)
Async XLA Ops:
  0.0 10.2 %copy-start = (f32[384,128]{1,0:T(8,128)S(1)}, f32[384,128]{1,0:T(8,128)}, u32[]{:S(2)}) copy-start(f32[384,128]{1,0:T(8,128)} %mer_ref.3) | copy-start | bytes 589828
  0.0 10.2 %copy-start.1 = (f32[16,48]{1,0:T(8,128)S(1)}, f32[16,48]{1,0:T(8,128)}, u32[]{:S(2)}) copy-start(f32[16,48]{1,0:T(8,128)} %zon_ref.3) | copy-start | bytes 9220
  5.4 17.5 %collective-permute-start = (f32[16,8,512]{2,1,0:T(8,128)}, f32[16,8,512]{2,1,0:T(8,128)S(1)}, u32[]{:S(2)}, u32[]{:S(2)}) collective-permute-start(f32[16,8,512]{2,1,0:T(8,128)} %get-tuple-element.35), channel_id=1, source_target_pairs={{0,16},{1,17},{2,18},{3,19},{4,20},{5,21},{6,22},{7,23},{8,24},{9,... | collective-permute-start | bytes 786440 | tf_op jit(solution)/shard_map/ppermute | solution.py:260
  7.1 16.0 %collective-permute-start.1 = (f32[16,8,512]{2,1,0:T(8,128)}, f32[16,8,512]{2,1,0:T(8,128)S(1)}, u32[]{:S(2)}, u32[]{:S(2)}) collective-permute-start(f32[16,8,512]{2,1,0:T(8,128)} %get-tuple-element.36), channel_id=1, source_target_pairs={{0,32},{1,33},{2,34},{3,35},{4,36},{5,37},{6,38},{7,39},{8,40},{9,... | collective-permute-start | bytes 786440 | tf_op jit(solution)/shard_map/ppermute | solution.py:260
  10.0 14.5 %collective-permute-start.2 = (f32[16,8,512]{2,1,0:T(8,128)}, f32[16,8,512]{2,1,0:T(8,128)S(1)}, u32[]{:S(2)}, u32[]{:S(2)}) collective-permute-start(f32[16,8,512]{2,1,0:T(8,128)} %get-tuple-element.37), channel_id=1, source_target_pairs={{0,48},{1,49},{2,50},{3,51},{4,52},{5,53},{6,54},{7,55},{8,56},{9,... | collective-permute-start | bytes 786440 | tf_op jit(solution)/shard_map/ppermute | solution.py:260
  18.3 22.5 %collective-permute-start.14 = (f32[16,8,768]{2,1,0:T(8,128)}, f32[16,8,768]{2,1,0:T(8,128)S(1)}, u32[]{:S(2)}, u32[]{:S(2)}) collective-permute-start(f32[16,8,768]{2,1,0:T(8,128)} %get-tuple-element.52), channel_id=1, source_target_pairs={{0,16},{1,17},{2,18},{3,19},{4,20},{5,21},{6,22},{7,23},{8,24},{9,... | collective-permute-start | bytes 1179656 | tf_op jit(solution)/shard_map/ppermute | solution.py:260
  18.8 23.1 %collective-permute-start.15 = (f32[16,8,768]{2,1,0:T(8,128)}, f32[16,8,768]{2,1,0:T(8,128)S(1)}, u32[]{:S(2)}, u32[]{:S(2)}) collective-permute-start(f32[16,8,768]{2,1,0:T(8,128)} %get-tuple-element.53), channel_id=1, source_target_pairs={{0,32},{1,33},{2,34},{3,35},{4,36},{5,37},{6,38},{7,39},{8,40},{9,... | collective-permute-start | bytes 1179656 | tf_op jit(solution)/shard_map/ppermute | solution.py:260
  22.9 1.6 %copy-start.2 = (f32[16,8,512]{2,1,0:T(8,128)}, f32[16,8,512]{2,1,0:T(8,128)S(1)}, u32[]{:S(2)}) copy-start(f32[16,8,512]{2,1,0:T(8,128)S(1)} %collective-permute-done.p1) | copy-start | bytes 786436
  22.9 22.6 %collective-permute-start.16 = (f32[16,8,768]{2,1,0:T(8,128)}, f32[16,8,768]{2,1,0:T(8,128)S(1)}, u32[]{:S(2)}, u32[]{:S(2)}) collective-permute-start(f32[16,8,768]{2,1,0:T(8,128)} %get-tuple-element.54), channel_id=1, source_target_pairs={{0,48},{1,49},{2,50},{3,51},{4,52},{5,53},{6,54},{7,55},{8,56},{9,... | collective-permute-start | bytes 1179656 | tf_op jit(solution)/shard_map/ppermute | solution.py:260
  23.1 1.4 %copy-start.3 = (f32[16,8,512]{2,1,0:T(8,128)}, f32[16,8,512]{2,1,0:T(8,128)S(1)}, u32[]{:S(2)}) copy-start(f32[16,8,512]{2,1,0:T(8,128)S(1)} %collective-permute-done.1.p2) | copy-start | bytes 786436
  24.5 0.7 copy-start.4
  27.6 6.3 %collective-permute-start.3 = (f32[2,4,8,512]{3,2,1,0:T(8,128)}, f32[2,4,8,512]{3,2,1,0:T(8,128)S(1)}, u32[]{:S(2)}, u32[]{:S(2)}) collective-permute-start(f32[2,4,8,512]{3,2,1,0:T(8,128)} %get-tuple-element.39), channel_id=1, source_target_pairs={{0,128},{1,129},{2,130},{3,131},{4,132},{5,133},{6,134},{7,135},{8... | collective-permute-start | bytes 393224 | tf_op jit(solution)/shard_map/ppermute | solution.py:297
  28.8 11.2 %collective-permute-start.4 = (f32[2,4,8,512]{3,2,1,0:T(8,128)}, f32[2,4,8,512]{3,2,1,0:T(8,128)S(1)}, u32[]{:S(2)}, u32[]{:S(2)}) collective-permute-start(f32[2,4,8,512]{3,2,1,0:T(8,128)} %get-tuple-element.40), channel_id=1, source_target_pairs={{0,1},{1,0},{2,3},{3,2},{4,5},{5,4},{6,7},{7,6},{8,9},{9,8},{10,11... | collective-permute-start | bytes 393224 | tf_op jit(solution)/shard_map/ppermute | solution.py:297
  33.9 15.9 %copy-start.6 = (f32[2,4,8,512]{3,2,1,0:T(8,128)}, f32[2,4,8,512]{3,2,1,0:T(8,128)S(1)}, u32[]{:S(2)}) copy-start(f32[2,4,8,512]{3,2,1,0:T(8,128)S(1)} %collective-permute-done.3.refs_1_) | copy-start | bytes 393220
  33.9 25.0 %collective-permute-start.5 = (f32[2,4,8,512]{3,2,1,0:T(8,128)}, f32[2,4,8,512]{3,2,1,0:T(8,128)S(1)}, u32[]{:S(2)}, u32[]{:S(2)}) collective-permute-start(f32[2,4,8,512]{3,2,1,0:T(8,128)} %get-tuple-element.41), channel_id=1, source_target_pairs={{0,3},{1,2},{2,1},{3,0},{4,7},{5,6},{6,5},{7,4},{8,11},{9,10},{10,... | collective-permute-start | bytes 393224 | tf_op jit(solution)/shard_map/ppermute | solution.py:297
  40.1 9.8 %copy-start.7 = (f32[2,4,8,512]{3,2,1,0:T(8,128)}, f32[2,4,8,512]{3,2,1,0:T(8,128)S(1)}, u32[]{:S(2)}) copy-start(f32[2,4,8,512]{3,2,1,0:T(8,128)S(1)} %collective-permute-done.4.refs_2_) | copy-start | bytes 393220
  40.1 18.8 %collective-permute-start.6 = (f32[2,4,8,512]{3,2,1,0:T(8,128)}, f32[2,4,8,512]{3,2,1,0:T(8,128)S(1)}, u32[]{:S(2)}, u32[]{:S(2)}) collective-permute-start(f32[2,4,8,512]{3,2,1,0:T(8,128)} %get-tuple-element.42), channel_id=1, source_target_pairs={{0,131},{1,130},{2,129},{3,128},{4,135},{5,134},{6,133},{7,132},{8... | collective-permute-start | bytes 393224 | tf_op jit(solution)/shard_map/ppermute | solution.py:297
  40.9 18.1 %collective-permute-start.7 = (f32[2,4,8,512]{3,2,1,0:T(8,128)}, f32[2,4,8,512]{3,2,1,0:T(8,128)S(1)}, u32[]{:S(2)}, u32[]{:S(2)}) collective-permute-start(f32[2,4,8,512]{3,2,1,0:T(8,128)} %get-tuple-element.43), channel_id=1, source_target_pairs={{0,129},{1,128},{2,131},{3,130},{4,133},{5,132},{6,135},{7,134},{8... | collective-permute-start | bytes 393224 | tf_op jit(solution)/shard_map/ppermute | solution.py:297
  41.9 18.6 %collective-permute-start.8 = (f32[2,4,8,512]{3,2,1,0:T(8,128)}, f32[2,4,8,512]{3,2,1,0:T(8,128)S(1)}, u32[]{:S(2)}, u32[]{:S(2)}) collective-permute-start(f32[2,4,8,512]{3,2,1,0:T(8,128)} %get-tuple-element.44), channel_id=1, source_target_pairs={{0,130},{1,131},{2,128},{3,129},{4,134},{5,135},{6,132},{7,133},{8... | collective-permute-start | bytes 393224 | tf_op jit(solution)/shard_map/ppermute | solution.py:297
  45.5 15.1 %collective-permute-start.9 = (f32[2,4,8,512]{3,2,1,0:T(8,128)}, f32[2,4,8,512]{3,2,1,0:T(8,128)S(1)}, u32[]{:S(2)}, u32[]{:S(2)}) collective-permute-start(f32[2,4,8,512]{3,2,1,0:T(8,128)} %get-tuple-element.45), channel_id=1, source_target_pairs={{0,2},{1,3},{2,0},{3,1},{4,6},{5,7},{6,4},{7,5},{8,10},{9,11},{10,... | collective-permute-start | bytes 393224 | tf_op jit(solution)/shard_map/ppermute | solution.py:297
  49.9 48.9 %all-to-all-start = ((f32[64,8,768]{2,1,0:T(8,128)}), f32[64,8,768]{2,1,0:T(8,128)}, u32[]{:S(2)}, u32[]{:S(2)}) async-start(f32[64,8,768]{2,1,0:T(8,128)} %pad_maximum_fusion), calls=%async_computation | async-start | bytes 3145728 | tf_op jit(solution)/shard_map/all_to_all | solution.py:300
  58.9 1.7 %copy-start.8 = (f32[2,4,8,512]{3,2,1,0:T(8,128)}, f32[2,4,8,512]{3,2,1,0:T(8,128)S(1)}, u32[]{:S(2)}) copy-start(f32[2,4,8,512]{3,2,1,0:T(8,128)S(1)} %collective-permute-done.5.refs_3_) | copy-start | bytes 393220
  58.9 1.6 %copy-start.9 = (f32[2,4,8,512]{3,2,1,0:T(8,128)}, f32[2,4,8,512]{3,2,1,0:T(8,128)S(1)}, u32[]{:S(2)}) copy-start(f32[2,4,8,512]{3,2,1,0:T(8,128)S(1)} %collective-permute-done.6.refs_4_) | copy-start | bytes 393220
  58.9 1.6 %copy-start.10 = (f32[2,4,8,512]{3,2,1,0:T(8,128)}, f32[2,4,8,512]{3,2,1,0:T(8,128)S(1)}, u32[]{:S(2)}) copy-start(f32[2,4,8,512]{3,2,1,0:T(8,128)S(1)} %collective-permute-done.7.refs_5_) | copy-start | bytes 393220
  60.5 0.7 copy-start.11
  60.5 0.7 copy-start.12
  63.5 6.8 %copy-start.5 = (f32[8,2,8,512]{3,2,1,0:T(8,128)S(1)}, f32[8,2,8,512]{3,2,1,0:T(8,128)}, u32[]{:S(2)}) copy-start(f32[8,2,8,512]{3,2,1,0:T(8,128)} %get-tuple-element.49) | copy-start | bytes 786436
  64.5 15.7 %collective-permute-start.11 = (f32[8,2,8,512]{3,2,0,1:T(8,128)S(1)}, f32[8,2,8,512]{3,2,0,1:T(8,128)S(1)}, u32[]{:S(2)}, u32[]{:S(2)}) collective-permute-start(f32[8,2,8,512]{3,2,0,1:T(8,128)S(1)} %copy.6), channel_id=1, source_target_pairs={{0,8},{1,9},{2,10},{3,11},{4,12},{5,13},{6,14},{7,15},{8,0},{9,1},... | collective-permute-start | bytes 786440 | tf_op jit(solution)/shard_map/ppermute | solution.py:260
  68.6 18.9 %collective-permute-start.10 = (f32[8,2,8,512]{3,2,0,1:T(8,128)S(1)}, f32[8,2,8,512]{3,2,0,1:T(8,128)S(1)}, u32[]{:S(2)}, u32[]{:S(2)}) collective-permute-start(f32[8,2,8,512]{3,2,0,1:T(8,128)S(1)} %copy.5), channel_id=1, source_target_pairs={{0,4},{1,5},{2,6},{3,7},{4,0},{5,1},{6,2},{7,3},{8,12},{9,13},{10,... | collective-permute-start | bytes 786440 | tf_op jit(solution)/shard_map/ppermute | solution.py:260
  70.3 18.3 %collective-permute-start.12 = (f32[8,2,8,512]{3,2,1,0:T(8,128)S(1)}, f32[8,2,8,512]{3,2,1,0:T(8,128)S(1)}, u32[]{:S(2)}, u32[]{:S(2)}) collective-permute-start(f32[8,2,8,512]{3,2,1,0:T(8,128)S(1)} %copy-done.5), channel_id=1, source_target_pairs={{0,12},{1,13},{2,14},{3,15},{4,8},{5,9},{6,10},{7,11},{8,4},{9,5},... | collective-permute-start | bytes 786440 | tf_op jit(solution)/shard_map/ppermute | solution.py:260
  88.6 2.0 %collective-permute-start.13 = (f32[16,2,8,512]{3,2,1,0:T(8,128)S(1)}, f32[16,2,8,512]{3,2,1,0:T(8,128)S(1)}, u32[]{:S(2)}, u32[]{:S(2)}) collective-permute-start(f32[16,2,8,512]{3,2,1,0:T(8,128)S(1)} %bitcast.25), channel_id=1, source_target_pairs={{0,64},{1,65},{2,66},{3,67},{4,68},{5,69},{6,70},{7,71},{8,72},{9,... | collective-permute-start | bytes 1572872 | tf_op jit(solution)/shard_map/ppermute | solution.py:303
